TPU v7x, 1024 devices: a whole 8x8x8 slice. The times are simulated.
1024 devices in a mesh: seq: 16 (over x, z_lo), inner: 64 (over y, z_hi, core).
Axes of the slice: x: 8, y: 8, z: 8 (z_hi: 4, z_lo: 2; z = z_hi * 2 + z_lo), core: 2. Of those that a mesh axis runs over, the one named last changes fastest.
Arguments:
- queries: bfloat16 [16384, 8192], P('seq', 'inner'), may hold values from -6 to 6
- key_vectors: bfloat16 [16384, 8192], P('seq', 'inner'), may hold values from -6 to 6
- value_vectors: bfloat16 [16384, 8192], P('seq', 'inner'), may hold values from -6 to 6
- out_grad: bfloat16 [16384, 8192], P('seq', 'inner'), may hold values from -6 to 6
Outputs:
- attended: bfloat16 [16384, 8192], P('seq', 'inner')
- query_grad: bfloat16 [16384, 8192], P('seq', 'inner')
- key_grad: bfloat16 [16384, 8192], P('seq', 'inner')
- value_grad: bfloat16 [16384, 8192], P('seq', 'inner')
All inputs are finite; a program needn't handle non-finite values.
Results may differ from a plain program's by a relative error of at most 0.0058.
Values sent between devices are 32-bit elements; how exact they have to be, the bound alone decides.
No kernel may reach another device: no remote copies, remote signals or barrier semaphores. Data moves between devices by JAX's collectives and lax.ppermute only.
A program may use at most 32 MiB of HBM per device.

v0:
```python
import jax
import jax.numpy as jnp
from jax import lax
from jax.sharding import PartitionSpec as P

BLOCK = 512


def from_partner(value, axis, bit):
    mask = 2**bit
    pairs = [(source, source ^ mask) for source in range(lax.axis_size(axis))]
    return lax.ppermute(value, axis, pairs)


def prefix(part, axis, combine, identity, reverse):
    count = lax.axis_size(axis)
    place = lax.axis_index(axis)
    ahead = count - 1 - place if reverse else place
    gathered = lax.all_gather(part, axis)
    state = jnp.zeros_like(part) + jnp.asarray(identity, part.dtype)

    def one(step, state):
        source = count - 1 - step if reverse else step
        return combine(state, lax.dynamic_index_in_dim(gathered, source, 0, False))

    return lax.fori_loop(0, ahead, one, state)


def add_states(earlier, later):
    return jax.tree.map(jnp.add, earlier, later)


def per_device(queries, key_vectors, value_vectors, out_grad):
    half_rows, width = queries.shape
    count = half_rows // BLOCK
    side = lax.axis_index("inner") % 2
    is_second = side == 1
    position = (
        lax.axis_index("seq") * 2 * half_rows + side * half_rows + jnp.arange(half_rows)
    ).astype(jnp.float32)
    scaling = 1.0 / jnp.sqrt(width * (position + 1.0))
    scaled_grad = (scaling[:, None] * out_grad.astype(jnp.float32)).astype(jnp.bfloat16)
    scale_blocks = scaling.reshape(count, BLOCK)
    query_b = queries.reshape(count, BLOCK, width)
    key_b = key_vectors.reshape(count, BLOCK, width)
    value_b = value_vectors.reshape(count, BLOCK, width)
    grad_b = scaled_grad.reshape(count, BLOCK, width)
    outer_kv = jnp.einsum("nbd,nbv->ndv", key_b, value_b, preferred_element_type=jnp.float32)
    outer_back = jnp.einsum("nbd,nbv->ndv", query_b, grad_b, preferred_element_type=jnp.float32)
    local_kv = jnp.sum(outer_kv, 0)
    local_back = jnp.sum(outer_back, 0)
    zero_state = jnp.zeros_like(local_kv)
    other_kv, other_back = from_partner((local_kv, local_back), "inner", 0)
    earlier = prefix(local_kv + other_kv, "seq", add_states, zero_state, False)
    later = prefix(local_back + other_back, "seq", add_states, zero_state, True)
    state_in = earlier + jnp.where(is_second, other_kv, 0.0)
    back_in = later + jnp.where(is_second, 0.0, other_back)
    kv_used = (state_in[None] + jnp.cumsum(outer_kv, 0) - outer_kv).astype(jnp.bfloat16)
    back_used = (back_in[None] + (local_back[None] - jnp.cumsum(outer_back, 0))).astype(
        jnp.bfloat16
    )
    row_ids = jnp.arange(BLOCK)
    causal = (row_ids[:, None] >= row_ids[None, :])[None]
    scores = jnp.einsum("nbd,ncd->nbc", query_b, key_b, preferred_element_type=jnp.float32)
    weights = jnp.where(causal, scores, 0.0).astype(jnp.bfloat16)
    local = jnp.einsum("nbc,ncv->nbv", weights, value_b, preferred_element_type=jnp.float32)
    carried = jnp.einsum("nbd,ndv->nbv", query_b, kv_used, preferred_element_type=jnp.float32)
    attended = ((local + carried) * scale_blocks[..., None]).astype(jnp.bfloat16)
    grad_scores = jnp.where(
        causal, jnp.einsum("nbv,ncv->nbc", grad_b, value_b, preferred_element_type=jnp.float32), 0.0
    ).astype(jnp.bfloat16)
    query_grad = jnp.einsum(
        "nbc,ncd->nbd", grad_scores, key_b, preferred_element_type=jnp.float32
    ) + jnp.einsum("nbv,ndv->nbd", grad_b, kv_used, preferred_element_type=jnp.float32)
    key_grad = jnp.einsum(
        "nbc,nbd->ncd", grad_scores, query_b, preferred_element_type=jnp.float32
    ) + jnp.einsum("ncv,ndv->ncd", value_b, back_used, preferred_element_type=jnp.float32)
    value_grad = jnp.einsum(
        "nbc,nbv->ncv", weights, grad_b, preferred_element_type=jnp.float32
    ) + jnp.einsum("ncd,ndv->ncv", key_b, back_used, preferred_element_type=jnp.float32)
    shape = (half_rows, width)
    return (
        attended.reshape(shape),
        query_grad.astype(jnp.bfloat16).reshape(shape),
        key_grad.astype(jnp.bfloat16).reshape(shape),
        value_grad.astype(jnp.bfloat16).reshape(shape),
    )


def solution(mesh):
    return jax.shard_map(
        per_device,
        mesh=mesh,
        in_specs=(P("seq", "inner"), P("seq", "inner"), P("seq", "inner"), P("seq", "inner")),
        out_specs=(P("seq", "inner"), P("seq", "inner"), P("seq", "inner"), P("seq", "inner")),
        check_vma=False,
    )
```

profile of v0, /device:TPU:14, one launch (start us, length us, event | category | flops | bytes accessed | tf_op | source)
XLA Modules:
  0.0 204.6 jit_solution(2189670709589888734)
XLA Ops:
  7.2 0.0 all-gather.7.cloned.1.call-start
  7.3 1.2 multiply_convert_fusion
  8.5 0.9 fusion.6
  9.4 0.1 copy.41
  9.5 1.9 collective-permute-start.1
  11.5 1.2 collective-permute-done.1
  12.7 0.6 add.125
  13.3 0.0 all-gather.7.cloned.1.call-update
  13.3 0.0 all-gather.5.cloned.1.call-start
  13.4 0.3 fusion.5
  13.7 2.1 %collective-permute-start = (f32[128,128]{1,0:T(8,128)S(1)}, f32[128,128]{1,0:T(8,128)S(1)}, u32[]{:S(2)}, u32[]{:S(2)}) collective-permute-start(f32[128,128]{1,0:T(8,128)S(1)} %get-tuple-element.109), channel_id=1, source_target_pairs={{0,1},{1,0},{2,3},{3,2},{4,5},{5,4},{6,7},{7,6},{8,9},{9,8},{10,11... | collective-permute-start | bytes 196616 | tf_op jit(solution)/shard_map/ppermute | solution.py:12
  15.8 1.1 collective-permute-done
  16.8 0.6 copy-done.3
  17.5 0.6 add.111
  18.1 0.0 all-gather.5.cloned.1.call-update
  18.2 0.1 iota_compare_fusion
  18.2 0.5 select_convert_fusion
  18.7 0.5 select_convert_fusion.1
  19.2 79.4 %all-gather.7.cloned.1.call-done = f32[2048,128]{1,0:T(8,128)} async-done(((f32[128,128]{1,0:T(8,128)}), f32[2048,128]{1,0:T(8,128)}) %all-gather.7.cloned.1.call-update) | async-done | bytes 1048592 | tf_op jit(solution)/shard_map/all_gather | solution.py:19
  98.6 0.9 while.23
  98.6 0.9 bitcast_add_fusion.5
  99.5 77.6 %all-gather.5.cloned.1.call-done = f32[2048,128]{1,0:T(8,128)} async-done(((f32[128,128]{1,0:T(8,128)}), f32[2048,128]{1,0:T(8,128)}) %all-gather.5.cloned.1.call-update) | async-done | bytes 1048592 | tf_op jit(solution)/shard_map/all_gather | solution.py:19
  177.1 12.3 %while.22 = (s32[]{:T(128)}, f32[128,128]{1,0:T(8,128)S(1)}, s32[]{:T(128)}, f32[16,128,128]{2,1,0:T(8,128)}, s32[]{:T(128)}, /*index=5*/s32[]{:T(128)}, s32[]{:T(128)}) while((s32[]{:T(128)}, f32[128,128]{1,0:T(8,128)S(1)}, s32[]{:T(128)}, f32[16,128,128]{2,1,0:T(8,128)}, s32[]{:T(128)}, /*index=5*/s32[]{:T(128)}, s32[]{:T(128)}) %tuple.58), condition=%wide.region_2.3_spmd, body=%wide.region_1.2_spmd.sunk | while | flops 16389 | bytes 196723 | solution.py:26
  177.1 0.9 bitcast_add_fusion.4
  178.0 0.9 bitcast_add_fusion.4
  178.9 0.9 bitcast_add_fusion.4
  179.7 0.9 bitcast_add_fusion.4
  180.6 0.9 bitcast_add_fusion.4
  181.5 0.9 bitcast_add_fusion.4
  182.4 0.9 bitcast_add_fusion.4
  183.3 0.9 bitcast_add_fusion.4
  184.2 0.9 bitcast_add_fusion.4
  185.0 0.9 bitcast_add_fusion.4
  185.9 0.9 bitcast_add_fusion.4
  186.8 0.9 bitcast_add_fusion.4
  187.7 0.9 bitcast_add_fusion.4
  188.6 0.9 bitcast_add_fusion.4
  189.4 0.7 select_add_fusion
  190.1 0.9 copy.42
  191.1 1.0 add_convert_fusion
  192.0 0.2 convolution_bitcast_fusion
  192.2 0.2 convolution_bitcast_fusion.2
  192.5 0.2 fusion.7
  192.8 0.2 convolution_bitcast_fusion.1
  193.0 1.2 fusion.2
  194.2 1.1 fusion.1
  195.3 1.2 fusion.3
  196.6 1.2 fusion.4
  (14 shorter events, 0.1 us)
Async XLA Ops:
  7.2 1.3 copy-start
  7.2 6.2 %copy-start.1 = (bf16[1024,128]{1,0:T(8,128)(2,1)S(1)}, bf16[1024,128]{1,0:T(8,128)(2,1)}, u32[]{:S(2)}) copy-start(bf16[1024,128]{1,0:T(8,128)(2,1)} %param.9) | copy-start | bytes 786436
  7.2 6.2 %copy-start.2 = (bf16[1024,128]{1,0:T(8,128)(2,1)S(1)}, bf16[1024,128]{1,0:T(8,128)(2,1)}, u32[]{:S(2)}) copy-start(bf16[1024,128]{1,0:T(8,128)(2,1)} %param.10) | copy-start | bytes 786436
  7.2 91.4 %all-gather.7.cloned.1.call-start = ((), (), s32[]{:S(2)}) async-start(), calls=%async_computation.1 | async-start | bytes 1114112 | tf_op jit(solution)/shard_map/all_gather | solution.py:19
  9.5 3.1 %collective-permute-start.1 = (f32[128,128]{1,0:T(8,128)S(1)}, f32[128,128]{1,0:T(8,128)S(1)}, u32[]{:S(2)}, u32[]{:S(2)}) collective-permute-start(f32[128,128]{1,0:T(8,128)S(1)} %copy.41), channel_id=1, source_target_pairs={{0,1},{1,0},{2,3},{3,2},{4,5},{5,4},{6,7},{7,6},{8,9},{9,8},{10,11... | collective-permute-start | bytes 196616 | tf_op jit(solution)/shard_map/ppermute | solution.py:12
  13.3 163.7 %all-gather.5.cloned.1.call-start = ((), (), s32[]{:S(2)}) async-start(), calls=%async_computation | async-start | bytes 1114112 | tf_op jit(solution)/shard_map/all_gather | solution.py:19
  13.7 3.1 %collective-permute-start = (f32[128,128]{1,0:T(8,128)S(1)}, f32[128,128]{1,0:T(8,128)S(1)}, u32[]{:S(2)}, u32[]{:S(2)}) collective-permute-start(f32[128,128]{1,0:T(8,128)S(1)} %get-tuple-element.109), channel_id=1, source_target_pairs={{0,1},{1,0},{2,3},{3,2},{4,5},{5,4},{6,7},{7,6},{8,9},{9,8},{10,11... | collective-permute-start | bytes 196616 | tf_op jit(solution)/shard_map/ppermute | solution.py:12
  16.8 0.6 copy-start.3
  191.1 1.4 copy-start.4
Sparse Core Ops, SparseCore 0:
  13.5 85.0 all-gather.6
  101.8 75.2 all-gather.4
where the time goes:
time: 206 us; the launch traced here: 205 us
  waiting for transfers between devices  159 us (77%)
  other arithmetic  17.1 us (8%)
  between operations  14.3 us (7%)
  matrix products  7.78 us (4%)
  starting transfers between devices  4.06 us (2%)
    all_gather x2, waiting for transfers between devices, prefix(): gathered = lax.all_gather(part, axis)  157 us
    add x15, other arithmetic, add_states(): return jax.tree.map(jnp.add, earlier, later)  12.8 us
  transfers between devices with their start and end apart: 4, of which 4 were waited for; matrix products, arithmetic and copies ran while one was open for 1% of the time, Pallas kernels for 0%

commit v1 on v0

v1 whole, which is shorter than its diff:
```python
import functools

import jax
import jax.numpy as jnp
from jax import lax
from jax.experimental import pallas as pl
from jax.experimental.pallas import tpu as pltpu
from jax.sharding import PartitionSpec as P

BLOCK = 512
SUB = 256
AXES = ("seq", "inner")
F32 = jnp.float32
BF16 = jnp.bfloat16


def dot(a, b, ca, cb):
    return lax.dot_general(a, b, (((ca,), (cb,)), ((), ())), preferred_element_type=F32)


def scaling_of(start, rows, width):
    row = lax.broadcasted_iota(jnp.int32, (rows, width), 0)
    position = (start + row).astype(F32)
    return 1.0 / jnp.sqrt(width * (position + 1.0))


def first_position(half_rows):
    return (lax.axis_index("seq") * 2 + lax.axis_index("inner") % 2) * half_rows


def outer_kernel(q_ref, k_ref, v_ref, o_ref, send_ref, keep_ref, grad_ref):
    half_rows, width = q_ref.shape
    start = first_position(half_rows)
    kv, back = [], []
    for b in range(half_rows // BLOCK):
        rows = pl.ds(b * BLOCK, BLOCK)
        scaling = scaling_of(start + b * BLOCK, BLOCK, width)
        grad = (scaling * o_ref[rows, :].astype(F32)).astype(BF16)
        grad_ref[rows, :] = grad
        kv.append(dot(k_ref[rows, :], v_ref[rows, :], 0, 0))
        back.append(dot(q_ref[rows, :], grad, 0, 0))
    keep_ref[:width, :] = kv[0]
    keep_ref[width:, :] = back[1]
    send_ref[:width, :] = kv[0] + kv[1]
    send_ref[width:, :] = back[0] + back[1]


def scan_kernel(parts_ref, out_ref):
    count = parts_ref.shape[0]
    me = lax.axis_index("seq") * 2 + lax.axis_index("inner") % 2
    is_kv = me < count // 2
    zero = jnp.zeros(parts_ref.shape[1:], F32)
    before = [zero]
    for i in range(count - 1):
        before.append(before[-1] + parts_ref[i])
    after = zero
    for i in reversed(range(count)):
        out_ref[i] = jnp.where(is_kv, before[i], after)
        after = after + parts_ref[i]


def main_kernel(q_ref, k_ref, v_ref, g_ref, state_ref, keep_ref, att_ref, qg_ref, kg_ref, vg_ref):
    half_rows, width = q_ref.shape
    start = first_position(half_rows)
    row = lax.broadcasted_iota(jnp.int32, (SUB, SUB), 0)
    col = lax.broadcasted_iota(jnp.int32, (SUB, SUB), 1)
    causal = row >= col
    kv0 = state_ref[:width, :]
    back1 = state_ref[width:, :]
    kv_used = [kv0.astype(BF16), (kv0 + keep_ref[:width, :]).astype(BF16)]
    back_used = [(back1 + keep_ref[width:, :]).astype(BF16), back1.astype(BF16)]
    for b in range(half_rows // BLOCK):
        tiles = [pl.ds(b * BLOCK + i * SUB, SUB) for i in range(BLOCK // SUB)]
        n = len(tiles)
        q = [q_ref[t, :] for t in tiles]
        k = [k_ref[t, :] for t in tiles]
        v = [v_ref[t, :] for t in tiles]
        g = [g_ref[t, :] for t in tiles]
        att = [dot(q[i], kv_used[b], 1, 0) for i in range(n)]
        qg = [dot(g[i], kv_used[b], 1, 1) for i in range(n)]
        kg = [dot(v[i], back_used[b], 1, 1) for i in range(n)]
        vg = [dot(k[i], back_used[b], 1, 0) for i in range(n)]
        for i in range(n):
            for j in range(i + 1):
                w = dot(q[i], k[j], 1, 1)
                s = dot(g[i], v[j], 1, 1)
                if i == j:
                    w = jnp.where(causal, w, 0.0)
                    s = jnp.where(causal, s, 0.0)
                w = w.astype(BF16)
                s = s.astype(BF16)
                att[i] = att[i] + dot(w, v[j], 1, 0)
                qg[i] = qg[i] + dot(s, k[j], 1, 0)
                kg[j] = kg[j] + dot(s, q[i], 0, 0)
                vg[j] = vg[j] + dot(w, g[i], 0, 0)
        for i in range(n):
            scaling = scaling_of(start + b * BLOCK + i * SUB, SUB, width)
            att_ref[tiles[i], :] = (att[i] * scaling).astype(BF16)
            qg_ref[tiles[i], :] = qg[i].astype(BF16)
            kg_ref[tiles[i], :] = kg[i].astype(BF16)
            vg_ref[tiles[i], :] = vg[i].astype(BF16)


def call(kernel, outs, limit):
    return pl.pallas_call(
        kernel,
        out_shape=outs,
        compiler_params=pltpu.CompilerParams(vmem_limit_bytes=limit),
    )


def per_device(groups, queries, key_vectors, value_vectors, out_grad):
    half_rows, width = queries.shape
    rows16 = jax.ShapeDtypeStruct((half_rows, width), BF16)
    states = jax.ShapeDtypeStruct((2 * width, width), F32)
    send, keep, grad = call(outer_kernel, (states, states, rows16), 2**24)(
        queries, key_vectors, value_vectors, out_grad
    )
    count = len(groups[0])
    parts = send.reshape(count, 2 * width // count, width)
    parts = lax.all_to_all(parts, AXES, 0, 0, axis_index_groups=groups)
    parts = call(scan_kernel, jax.ShapeDtypeStruct(parts.shape, F32), 2**23)(parts)
    parts = lax.all_to_all(parts, AXES, 0, 0, axis_index_groups=groups)
    state = parts.reshape(2 * width, width)
    return call(main_kernel, (rows16,) * 4, 2**24)(
        queries, key_vectors, value_vectors, grad, state, keep
    )


def solution(mesh):
    n_seq, n_inner = mesh.shape["seq"], mesh.shape["inner"]
    groups = [
        [s * n_inner + 2 * h + side for s in range(n_seq) for side in range(2)]
        for h in range(n_inner // 2)
    ]
    spec = P("seq", "inner")
    return jax.shard_map(
        functools.partial(per_device, groups),
        mesh=mesh,
        in_specs=(spec,) * 4,
        out_specs=(spec,) * 4,
        check_vma=False,
    )
```

time: 206 us -> 47.1 us (0.23)
  the two profiles are of different devices: /device:TPU:14 before, /device:TPU:1 now
where the time goes in v1:
time: 47.1 us; the launch traced here: 46.8 us
  blocking collectives  38.7 us (82%)
  local copies, waits for them, and re-layouts  3.79 us (8%)
  Pallas kernels  3.64 us (8%)
  between operations  0.66 us (1%)
    all_to_all x2, blocking collectives, per_device(): parts = lax.all_to_all(parts, AXES, 0, 0, axis_index_groups=groups)  38.7 us
    unnamed x8, local copies, waits for them, and re-layouts  3.79 us
    pallas_call x1, Pallas kernels, per_device(): call(main_kernel, (rows16,) * 4, 2 ** 24)  3.04 us

profile of v1, /device:TPU:1, one launch (start us, length us, event | category | flops | bytes accessed | tf_op | source)
XLA Modules:
  0.0 46.8 jit_solution(5352670513729936572)
XLA Ops:
  0.6 0.0 copy-start
  0.6 0.9 %copy-done = bf16[1024,128]{1,0:T(8,128)(2,1)S(1)} copy-done((bf16[1024,128]{1,0:T(8,128)(2,1)S(1)}, bf16[1024,128]{1,0:T(8,128)(2,1)}, u32[]{:S(2)}) %copy-start) | copy-done | bytes 262168
  1.6 0.0 copy-start.1
  1.6 0.9 %copy-done.1 = bf16[1024,128]{1,0:T(8,128)(2,1)S(1)} copy-done((bf16[1024,128]{1,0:T(8,128)(2,1)S(1)}, bf16[1024,128]{1,0:T(8,128)(2,1)}, u32[]{:S(2)}) %copy-start.1) | copy-done | bytes 262168
  2.5 0.0 copy-start.2
  2.5 0.9 %copy-done.2 = bf16[1024,128]{1,0:T(8,128)(2,1)S(1)} copy-done((bf16[1024,128]{1,0:T(8,128)(2,1)S(1)}, bf16[1024,128]{1,0:T(8,128)(2,1)}, u32[]{:S(2)}) %copy-start.2) | copy-done | bytes 262168
  3.5 0.0 copy-start.3
  3.5 0.9 %copy-done.3 = bf16[1024,128]{1,0:T(8,128)(2,1)S(1)} copy-done((bf16[1024,128]{1,0:T(8,128)(2,1)S(1)}, bf16[1024,128]{1,0:T(8,128)(2,1)}, u32[]{:S(2)}) %copy-start.3) | copy-done | bytes 262168
  4.4 0.6 %shard_map.75 = (f32[256,128]{1,0:T(8,128)S(1)}, f32[256,128]{1,0:T(8,128)S(1)}, bf16[1024,128]{1,0:T(8,128)(2,1)S(1)}) custom-call(bf16[1024,128]{1,0:T(8,128)(2,1)S(1)} %copy-done, bf16[1024,128]{1,0:T(8,128)(2,1)S(1)} %copy-done.1, bf16[1024,128]{1,0:T(8,128)(2,1)S(1)} %copy-done.2, bf16[1024,128]{1,0:T(8,128)(2,1)S(1)} %copy-done.3), custom_call_target="tpu_custom_call" | custom-call | tf_op jit(solution)/shard_map/pallas_call | solution.py:116
  5.0 26.2 %all_to_all.10.parts_ref = f32[32,8,128]{2,1,0:T(8,128)S(1)} all-to-all(f32[32,8,128]{2,1,0:T(8,128)S(1)} %bitcast.3), channel_id=1, replica_groups={{0,1,64,65,128,129,192,193,256,257,320,321,384,385,448,449,512,513,576,..., dimensions={0} | all-to-all | bytes 262144 | tf_op jit(solution)/shard_map/all_to_all | solution.py:121
  31.3 12.5 %all_to_all.11 = f32[32,8,128]{2,1,0:T(8,128)S(1)} all-to-all(f32[32,8,128]{2,1,0:T(8,128)S(1)} %shard_map.76), channel_id=1, replica_groups={{0,1,64,65,128,129,192,193,256,257,320,321,384,385,448,449,512,513,576,..., dimensions={0} | all-to-all | bytes 262144 | tf_op jit(solution)/shard_map/all_to_all | solution.py:123
  43.8 3.0 %shard_map.77 = (bf16[1024,128]{1,0:T(8,128)(2,1)}, bf16[1024,128]{1,0:T(8,128)(2,1)}, bf16[1024,128]{1,0:T(8,128)(2,1)}, bf16[1024,128]{1,0:T(8,128)(2,1)}) custom-call(bf16[1024,128]{1,0:T(8,128)(2,1)S(1)} %copy-done, bf16[1024,128]{1,0:T(8,128)(2,1)S(1)} %copy-done.1, bf16[1024,128]{1,0:T(8,128)(2,1)S(1)} %copy-done.2, ...), custom_call_target="tpu_custom_call" | custom-call | tf_op jit(solution)/shard_map/pallas_call | solution.py:125
  (1 shorter events, 0.0 us)
Async XLA Ops:
  0.6 1.0 %copy-start = (bf16[1024,128]{1,0:T(8,128)(2,1)S(1)}, bf16[1024,128]{1,0:T(8,128)(2,1)}, u32[]{:S(2)}) copy-start(bf16[1024,128]{1,0:T(8,128)(2,1)} %q_ref.3) | copy-start | bytes 786436
  1.6 0.9 %copy-start.1 = (bf16[1024,128]{1,0:T(8,128)(2,1)S(1)}, bf16[1024,128]{1,0:T(8,128)(2,1)}, u32[]{:S(2)}) copy-start(bf16[1024,128]{1,0:T(8,128)(2,1)} %k_ref.3) | copy-start | bytes 786436
  2.5 0.9 %copy-start.2 = (bf16[1024,128]{1,0:T(8,128)(2,1)S(1)}, bf16[1024,128]{1,0:T(8,128)(2,1)}, u32[]{:S(2)}) copy-start(bf16[1024,128]{1,0:T(8,128)(2,1)} %v_ref.3) | copy-start | bytes 786436
  3.5 0.9 %copy-start.3 = (bf16[1024,128]{1,0:T(8,128)(2,1)S(1)}, bf16[1024,128]{1,0:T(8,128)(2,1)}, u32[]{:S(2)}) copy-start(bf16[1024,128]{1,0:T(8,128)(2,1)} %o_ref.1) | copy-start | bytes 786436

commit v2 on v1

--- a/solution.py
+++ b/solution.py
@@ -28,16 +28,32 @@
     return (lax.axis_index("seq") * 2 + lax.axis_index("inner") % 2) * half_rows
 
 
-def outer_kernel(q_ref, k_ref, v_ref, o_ref, send_ref, keep_ref, grad_ref):
+def outer_kernel(
+    q_hbm, k_hbm, v_hbm, o_hbm, send_ref, keep_ref, q_ref, k_ref, v_ref, grad_ref, o_ref, sems
+):
     half_rows, width = q_ref.shape
     start = first_position(half_rows)
+    pairs = ((k_hbm, k_ref), (v_hbm, v_ref), (o_hbm, o_ref), (q_hbm, q_ref))
+    copies = []
+    for b in range(half_rows // BLOCK):
+        rows = pl.ds(b * BLOCK, BLOCK)
+        for i, (source, target) in enumerate(pairs):
+            copies.append(
+                pltpu.make_async_copy(source.at[rows, :], target.at[rows, :], sems.at[b, i])
+            )
+    for copy in copies:
+        copy.start()
     kv, back = [], []
     for b in range(half_rows // BLOCK):
         rows = pl.ds(b * BLOCK, BLOCK)
         scaling = scaling_of(start + b * BLOCK, BLOCK, width)
+        copies[4 * b].wait()
+        copies[4 * b + 1].wait()
+        kv.append(dot(k_ref[rows, :], v_ref[rows, :], 0, 0))
+        copies[4 * b + 2].wait()
         grad = (scaling * o_ref[rows, :].astype(F32)).astype(BF16)
         grad_ref[rows, :] = grad
-        kv.append(dot(k_ref[rows, :], v_ref[rows, :], 0, 0))
+        copies[4 * b + 3].wait()
         back.append(dot(q_ref[rows, :], grad, 0, 0))
     keep_ref[:width, :] = kv[0]
     keep_ref[width:, :] = back[1]
@@ -59,16 +75,11 @@
         after = after + parts_ref[i]
 
 
-def main_kernel(q_ref, k_ref, v_ref, g_ref, state_ref, keep_ref, att_ref, qg_ref, kg_ref, vg_ref):
+def local_kernel(q_ref, k_ref, v_ref, g_ref, att_ref, qg_ref, kg_ref, vg_ref):
     half_rows, width = q_ref.shape
-    start = first_position(half_rows)
     row = lax.broadcasted_iota(jnp.int32, (SUB, SUB), 0)
     col = lax.broadcasted_iota(jnp.int32, (SUB, SUB), 1)
     causal = row >= col
-    kv0 = state_ref[:width, :]
-    back1 = state_ref[width:, :]
-    kv_used = [kv0.astype(BF16), (kv0 + keep_ref[:width, :]).astype(BF16)]
-    back_used = [(back1 + keep_ref[width:, :]).astype(BF16), back1.astype(BF16)]
     for b in range(half_rows // BLOCK):
         tiles = [pl.ds(b * BLOCK + i * SUB, SUB) for i in range(BLOCK // SUB)]
         n = len(tiles)
@@ -76,10 +87,7 @@
         k = [k_ref[t, :] for t in tiles]
         v = [v_ref[t, :] for t in tiles]
         g = [g_ref[t, :] for t in tiles]
-        att = [dot(q[i], kv_used[b], 1, 0) for i in range(n)]
-        qg = [dot(g[i], kv_used[b], 1, 1) for i in range(n)]
-        kg = [dot(v[i], back_used[b], 1, 1) for i in range(n)]
-        vg = [dot(k[i], back_used[b], 1, 0) for i in range(n)]
+        att, qg, kg, vg = ([0.0] * n for _ in range(4))
         for i in range(n):
             for j in range(i + 1):
                 w = dot(q[i], k[j], 1, 1)
@@ -94,37 +102,97 @@
                 kg[j] = kg[j] + dot(s, q[i], 0, 0)
                 vg[j] = vg[j] + dot(w, g[i], 0, 0)
         for i in range(n):
-            scaling = scaling_of(start + b * BLOCK + i * SUB, SUB, width)
-            att_ref[tiles[i], :] = (att[i] * scaling).astype(BF16)
-            qg_ref[tiles[i], :] = qg[i].astype(BF16)
-            kg_ref[tiles[i], :] = kg[i].astype(BF16)
-            vg_ref[tiles[i], :] = vg[i].astype(BF16)
-
-
-def call(kernel, outs, limit):
+            att_ref[tiles[i], :] = att[i]
+            qg_ref[tiles[i], :] = qg[i]
+            kg_ref[tiles[i], :] = kg[i]
+            vg_ref[tiles[i], :] = vg[i]
+
+
+def final_kernel(
+    q_ref, k_ref, v_ref, g_ref, state_ref, keep_ref,
+    att_in, qg_in, kg_in, vg_in,
+    att_hbm, qg_hbm, kg_hbm, vg_hbm,
+    att_ref, qg_ref, kg_ref, vg_ref, sems,
+):
+    half_rows, width = q_ref.shape
+    start = first_position(half_rows)
+    kv0 = state_ref[:width, :]
+    back1 = state_ref[width:, :]
+    kv_used = [kv0.astype(BF16), (kv0 + keep_ref[:width, :]).astype(BF16)]
+    back_used = [(back1 + keep_ref[width:, :]).astype(BF16), back1.astype(BF16)]
+    copies = []
+
+    def put(value, buffer, out, rows):
+        buffer[rows, :] = value.astype(BF16)
+        n = len(copies)
+        copy = pltpu.make_async_copy(buffer.at[rows, :], out.at[rows, :], sems.at[n])
+        copy.start()
+        copies.append(copy)
+
+    for b in range(half_rows // BLOCK):
+        rows = pl.ds(b * BLOCK, BLOCK)
+        q, k, v, g = q_ref[rows, :], k_ref[rows, :], v_ref[rows, :], g_ref[rows, :]
+        put(qg_in[rows, :] + dot(g, kv_used[b], 1, 1), qg_ref, qg_hbm, rows)
+        put(kg_in[rows, :] + dot(v, back_used[b], 1, 1), kg_ref, kg_hbm, rows)
+        put(vg_in[rows, :] + dot(k, back_used[b], 1, 0), vg_ref, vg_hbm, rows)
+        scaling = scaling_of(start + b * BLOCK, BLOCK, width)
+        put((att_in[rows, :] + dot(q, kv_used[b], 1, 0)) * scaling, att_ref, att_hbm, rows)
+    for copy in copies:
+        copy.wait()
+
+
+def in_memory(array):
+    return pltpu.with_memory_space_constraint(array, pltpu.HBM)
+
+
+def call(kernel, outs, limit, **options):
     return pl.pallas_call(
         kernel,
         out_shape=outs,
         compiler_params=pltpu.CompilerParams(vmem_limit_bytes=limit),
+        **options,
     )
 
 
 def per_device(groups, queries, key_vectors, value_vectors, out_grad):
     half_rows, width = queries.shape
+    blocks = half_rows // BLOCK
     rows16 = jax.ShapeDtypeStruct((half_rows, width), BF16)
+    rows32 = jax.ShapeDtypeStruct((half_rows, width), F32)
     states = jax.ShapeDtypeStruct((2 * width, width), F32)
-    send, keep, grad = call(outer_kernel, (states, states, rows16), 2**24)(
-        queries, key_vectors, value_vectors, out_grad
-    )
+    in_hbm = pl.BlockSpec(memory_space=pltpu.HBM)
+    send, keep, q, k, v, grad = call(
+        outer_kernel,
+        (states, states) + (rows16,) * 4,
+        2**23,
+        in_specs=[in_hbm] * 4,
+        scratch_shapes=[
+            pltpu.VMEM((half_rows, width), BF16),
+            pltpu.SemaphoreType.DMA((blocks, 4)),
+        ],
+    )(*(in_memory(x) for x in (queries, key_vectors, value_vectors, out_grad)))
     count = len(groups[0])
     parts = send.reshape(count, 2 * width // count, width)
     parts = lax.all_to_all(parts, AXES, 0, 0, axis_index_groups=groups)
+    local = call(
+        local_kernel,
+        (rows32,) * 4,
+        2**24,
+        cost_estimate=pl.CostEstimate(
+            flops=12 * half_rows * BLOCK * width, bytes_accessed=2**22, transcendentals=0
+        ),
+    )(q, k, v, grad)
     parts = call(scan_kernel, jax.ShapeDtypeStruct(parts.shape, F32), 2**23)(parts)
     parts = lax.all_to_all(parts, AXES, 0, 0, axis_index_groups=groups)
     state = parts.reshape(2 * width, width)
-    return call(main_kernel, (rows16,) * 4, 2**24)(
-        queries, key_vectors, value_vectors, grad, state, keep
-    )
+    return call(
+        final_kernel,
+        (rows16,) * 4,
+        2**24,
+        out_specs=(in_hbm,) * 4,
+        scratch_shapes=[pltpu.VMEM((half_rows, width), BF16)] * 4
+        + [pltpu.SemaphoreType.DMA((4 * blocks,))],
+    )(q, k, v, grad, state, keep, *local)
 
 
 def solution(mesh):

time: 47.1 us -> 44.5 us (0.945)
  blocking collectives: 38.7 us -> 26.2 us
  waiting for transfers between devices: 0 us -> 7.53 us
  starting transfers between devices: 0 us -> 3.96 us
  local copies, waits for them, and re-layouts: 3.79 us -> 0 us
  Pallas kernels: 3.64 us -> 5.92 us
    all_to_all x2 -> x1, blocking collectives: 38.7 us -> 26.2 us  [per_device(): parts = lax.all_to_all(parts, AXES, 0, 0, axis_index_groups=groups)]
    all_to_all x0 -> x1, waiting for transfers between devices: none -> 7.53 us  [per_device(): parts = lax.all_to_all(parts, AXES, 0, 0, axis_index_groups=groups)]
    all_to_all x0 -> x1, starting transfers between devices: none -> 3.96 us  [per_device(): parts = lax.all_to_all(parts, AXES, 0, 0, axis_index_groups=groups)]
    unnamed x8 -> x0, local copies, waits for them, and re-layouts: 3.79 us -> none
    pallas_call x2 -> x3, Pallas kernels: 3.61 us -> 5.23 us  [the longest x1 2.04 us: per_device(): call(outer_kernel, (states, states) + (rows16,) * 4, 2 ** 23, in_specs=[i...]
    pallas_call x1, Pallas kernels: 0.04 us -> 0.69 us  [per_device(): call(scan_kernel, jax.ShapeDtypeStruct(parts.shape, F32), 2 ** 23)(parts)]
  transfers between devices with their start and end apart: 0 -> 1, of which waited for: 0 -> 1; matrix products, arithmetic and copies ran while one was open for 0% -> 0% of each run, Pallas kernels for 0% -> 4%
where the time goes in v2:
time: 44.5 us; the launch traced here: 44.3 us
  blocking collectives  26.2 us (59%)
  waiting for transfers between devices  7.53 us (17%)
  Pallas kernels  5.92 us (13%)
  starting transfers between devices  3.96 us (9%)
  between operations  0.65 us (1%)
    all_to_all x1, blocking collectives, per_device(): parts = lax.all_to_all(parts, AXES, 0, 0, axis_index_groups=groups)  26.2 us
    all_to_all x1, waiting for transfers between devices, per_device(): parts = lax.all_to_all(parts, AXES, 0, 0, axis_index_groups=groups)  7.53 us
    all_to_all x1, starting transfers between devices, per_device(): parts = lax.all_to_all(parts, AXES, 0, 0, axis_index_groups=groups)  3.96 us
    pallas_call x1, Pallas kernels, per_device(): call(outer_kernel, (states, states) + (rows16,) * 4, 2 ** 23, in_specs=[i...  2.04 us
    pallas_call x1, Pallas kernels, per_device(): call(local_kernel, (rows32,) * 4, 2 ** 24, cost_estimate=pl.CostEstimate(...  1.93 us
    pallas_call x1, Pallas kernels, per_device(): call(final_kernel, (rows16,) * 4, 2 ** 24, out_specs=(in_hbm,) * 4, scrat...  1.27 us
  transfers between devices with their start and end apart: 1, of which 1 were waited for; matrix products, arithmetic and copies ran while one was open for 0% of the time, Pallas kernels for 4%

profile of v2, /device:TPU:1, one launch (start us, length us, event | category | flops | bytes accessed | tf_op | source)
XLA Modules:
  0.0 44.3 jit_solution(14734162728390116415)
XLA Ops:
  0.6 2.0 %shard_map.75 = (f32[256,128]{1,0:T(8,128)S(1)}, f32[256,128]{1,0:T(8,128)S(1)}, bf16[1024,128]{1,0:T(8,128)(2,1)S(1)}, bf16[1024,128]{1,0:T(8,128)(2,1)S(1)}, b...) custom-call(bf16[1024,128]{1,0:T(8,128)(2,1)} %q_hbm.1, bf16[1024,128]{1,0:T(8,128)(2,1)} %k_hbm.1, ...), custom_call_target="tpu_custom_call" | custom-call | tf_op jit(solution)/shard_map/pallas_call | solution.py:164
  2.7 26.2 %all_to_all.10.parts_ref = f32[32,8,128]{2,1,0:T(8,128)S(1)} all-to-all(f32[32,8,128]{2,1,0:T(8,128)S(1)} %bitcast.3), channel_id=1, replica_groups={{0,1,64,65,128,129,192,193,256,257,320,321,384,385,448,449,512,513,576,..., dimensions={0} | all-to-all | bytes 262144 | tf_op jit(solution)/shard_map/all_to_all | solution.py:176
  28.9 0.7 %shard_map.76 = f32[32,8,128]{2,1,0:T(8,128)} custom-call(f32[32,8,128]{2,1,0:T(8,128)S(1)} %all_to_all.10.parts_ref), custom_call_target="tpu_custom_call" | custom-call | tf_op jit(solution)/shard_map/pallas_call | solution.py:185
  29.6 4.0 %all-to-all-start.1 = ((f32[32,8,128]{2,1,0:T(8,128)}), f32[32,8,128]{2,1,0:T(8,128)S(1)}, u32[]{:S(2)}, u32[]{:S(2)}) async-start(f32[32,8,128]{2,1,0:T(8,128)} %shard_map.76), calls=%async_computation.1 | async-start | bytes 262144 | tf_op jit(solution)/shard_map/all_to_all | solution.py:186
  33.6 1.9 %shard_map.77 = (f32[1024,128]{1,0:T(8,128)S(1)}, f32[1024,128]{1,0:T(8,128)S(1)}, f32[1024,128]{1,0:T(8,128)S(1)}, f32[1024,128]{1,0:T(8,128)S(1)}) custom-call(bf16[1024,128]{1,0:T(8,128)(2,1)S(1)} %get-tuple-element.14.q_ref, bf16[1024,128]{1,0:T(8,128)(2,1)S(1)} %get-tuple-element.15.k_ref, bf16[1024,128]{1,0:T(8,128)(2,1)S(1)} %get-tuple-element.16.v_ref, ...), custom_call_target="tpu_custom_call" | custom-call | flops 805306368 | bytes 4194304 | tf_op jit(solution)/shard_map/pallas_call | solution.py:177
  35.5 7.5 %all-to-all-done.1 = f32[32,8,128]{2,1,0:T(8,128)S(1)} async-done(((f32[32,8,128]{2,1,0:T(8,128)}), f32[32,8,128]{2,1,0:T(8,128)S(1)}, u32[]{:S(2)}, u32[]{:S(2)}) %all-to-all-start.1) | async-done | bytes 131104 | tf_op jit(solution)/shard_map/all_to_all | solution.py:186
  43.0 1.3 %shard_map.78 = (bf16[1024,128]{1,0:T(8,128)(2,1)}, bf16[1024,128]{1,0:T(8,128)(2,1)}, bf16[1024,128]{1,0:T(8,128)(2,1)}, bf16[1024,128]{1,0:T(8,128)(2,1)}) custom-call(bf16[1024,128]{1,0:T(8,128)(2,1)S(1)} %get-tuple-element.14.q_ref, bf16[1024,128]{1,0:T(8,128)(2,1)S(1)} %get-tuple-element.15.k_ref, bf16[1024,128]{1,0:T(8,128)(2,1)S(1)} %get-tuple-element.16.v_ref, ...), custom_call_target="tpu_custom_call" | custom-call | tf_op jit(solution)/shard_map/pallas_call | solution.py:188
Async XLA Ops:
  29.6 13.4 %all-to-all-start.1 = ((f32[32,8,128]{2,1,0:T(8,128)}), f32[32,8,128]{2,1,0:T(8,128)S(1)}, u32[]{:S(2)}, u32[]{:S(2)}) async-start(f32[32,8,128]{2,1,0:T(8,128)} %shard_map.76), calls=%async_computation.1 | async-start | bytes 262144 | tf_op jit(solution)/shard_map/all_to_all | solution.py:186

commit v3 on v2

v3 whole, which is shorter than its diff:
```python
import functools

import jax
import jax.numpy as jnp
from jax import lax
from jax.experimental import pallas as pl
from jax.experimental.pallas import tpu as pltpu
from jax.sharding import PartitionSpec as P

BLOCK = 512
SUB = 256
AXES = ("seq", "inner")
F32 = jnp.float32
BF16 = jnp.bfloat16


def dot(a, b, ca, cb):
    return lax.dot_general(a, b, (((ca,), (cb,)), ((), ())), preferred_element_type=F32)


def scaling_of(start, rows, width):
    row = lax.broadcasted_iota(jnp.int32, (rows, width), 0)
    position = (start + row).astype(F32)
    return 1.0 / jnp.sqrt(width * (position + 1.0))


def first_position(half_rows):
    return (lax.axis_index("seq") * 2 + lax.axis_index("inner") % 2) * half_rows


def outer_kernel(
    q_hbm, k_hbm, v_hbm, o_hbm,
    send_ref, own_ref, keep_ref, q_ref, k_ref, v_ref, grad_ref,
    o_ref, total_ref, sems,
):
    half_rows, width = q_ref.shape
    start = first_position(half_rows)
    pairs = ((k_hbm, k_ref), (v_hbm, v_ref), (o_hbm, o_ref), (q_hbm, q_ref))
    copies = []
    for b in range(half_rows // BLOCK):
        rows = pl.ds(b * BLOCK, BLOCK)
        for i, (source, target) in enumerate(pairs):
            copies.append(
                pltpu.make_async_copy(source.at[rows, :], target.at[rows, :], sems.at[b, i])
            )
    for copy in copies:
        copy.start()
    kv, back = [], []
    for b in range(half_rows // BLOCK):
        rows = pl.ds(b * BLOCK, BLOCK)
        scaling = scaling_of(start + b * BLOCK, BLOCK, width)
        copies[4 * b].wait()
        copies[4 * b + 1].wait()
        kv.append(dot(k_ref[rows, :], v_ref[rows, :], 0, 0))
        copies[4 * b + 2].wait()
        grad = (scaling * o_ref[rows, :].astype(F32)).astype(BF16)
        grad_ref[rows, :] = grad
        copies[4 * b + 3].wait()
        back.append(dot(q_ref[rows, :], grad, 0, 0))
    keep_ref[:width, :] = kv[0]
    keep_ref[width:, :] = back[1]
    half = width // 2
    mine = lax.axis_index("inner") % 2
    for i, total in enumerate((kv[0] + kv[1], back[0] + back[1])):
        total_ref[...] = total
        own_ref[i] = total_ref[pl.ds(mine * half, half), :]
        send_ref[i] = total_ref[pl.ds((1 - mine) * half, half), :]


def spread_kernel(own_ref, got_ref, *refs):
    out_ref = refs[-1]
    me = lax.axis_index("seq")
    kv = own_ref[0] + got_ref[0]
    back = own_ref[1] + got_ref[1]
    for i in range(out_ref.shape[0]):
        out_ref[i] = jnp.where(i > me, kv, back)


def gather_kernel(parts_ref, own_ref, got_ref, send_ref, mine_ref):
    me = lax.axis_index("seq")
    is_second = lax.axis_index("inner") % 2 == 1
    zero = jnp.zeros(parts_ref.shape[1:], F32)
    earlier, later = zero, zero
    count = parts_ref.shape[0]
    for i in range(count):
        earlier = earlier + jnp.where(i < me, parts_ref[i], zero)
        j = count - 1 - i
        later = later + jnp.where(j > me, parts_ref[j], zero)
    send_ref[0] = earlier + jnp.where(is_second, zero, own_ref[0])
    send_ref[1] = later + jnp.where(is_second, own_ref[1], zero)
    mine_ref[0] = earlier + jnp.where(is_second, got_ref[0], zero)
    mine_ref[1] = later + jnp.where(is_second, zero, got_ref[1])


def local_kernel(b, q_ref, k_ref, v_ref, g_ref, *refs):
    outs = refs[-4:]
    row = lax.broadcasted_iota(jnp.int32, (SUB, SUB), 0)
    col = lax.broadcasted_iota(jnp.int32, (SUB, SUB), 1)
    causal = row >= col
    n = BLOCK // SUB
    tiles = [pl.ds(b * BLOCK + i * SUB, SUB) for i in range(n)]
    q, k, v, g = ([ref[t, :] for t in tiles] for ref in (q_ref, k_ref, v_ref, g_ref))
    att, qg, kg, vg = ([0.0] * n for _ in range(4))
    for i in range(n):
        for j in range(i + 1):
            w = dot(q[i], k[j], 1, 1)
            s = dot(g[i], v[j], 1, 1)
            if i == j:
                w = jnp.where(causal, w, 0.0)
                s = jnp.where(causal, s, 0.0)
            w = w.astype(BF16)
            s = s.astype(BF16)
            att[i] = att[i] + dot(w, v[j], 1, 0)
            qg[i] = qg[i] + dot(s, k[j], 1, 0)
            kg[j] = kg[j] + dot(s, q[i], 0, 0)
            vg[j] = vg[j] + dot(w, g[i], 0, 0)
    for out, parts in zip(outs, (att, qg, kg, vg)):
        for i in range(n):
            out[pl.ds(i * SUB, SUB), :] = parts[i]


def final_kernel(q_ref, k_ref, v_ref, g_ref, mine_ref, got_ref, keep_ref, *refs):
    local, outs = refs[:8], refs[8:12]
    buffers, state_ref, sems = refs[12:16], refs[16], refs[17]
    half_rows, width = q_ref.shape
    start = first_position(half_rows)
    half = width // 2
    mine = lax.axis_index("inner") % 2
    for i in range(2):
        state_ref[i, pl.ds(mine * half, half), :] = mine_ref[i]
        state_ref[i, pl.ds((1 - mine) * half, half), :] = got_ref[i]
    kv0 = state_ref[0]
    back1 = state_ref[1]
    kv_used = [kv0.astype(BF16), (kv0 + keep_ref[:width, :]).astype(BF16)]
    back_used = [(back1 + keep_ref[width:, :]).astype(BF16), back1.astype(BF16)]
    copies = []

    def put(i, value, rows):
        buffers[i][rows, :] = value.astype(BF16)
        copy = pltpu.make_async_copy(
            buffers[i].at[rows, :], outs[i].at[rows, :], sems.at[len(copies)]
        )
        copy.start()
        copies.append(copy)

    for b in range(half_rows // BLOCK):
        rows = pl.ds(b * BLOCK, BLOCK)
        q, k, v, g = q_ref[rows, :], k_ref[rows, :], v_ref[rows, :], g_ref[rows, :]
        att, qg, kg, vg = (ref[...] for ref in local[4 * b : 4 * b + 4])
        put(1, qg + dot(g, kv_used[b], 1, 1), rows)
        put(2, kg + dot(v, back_used[b], 1, 1), rows)
        put(3, vg + dot(k, back_used[b], 1, 0), rows)
        scaling = scaling_of(start + b * BLOCK, BLOCK, width)
        put(0, (att + dot(q, kv_used[b], 1, 0)) * scaling, rows)
    for copy in copies:
        copy.wait()


def in_memory(array):
    return pltpu.with_memory_space_constraint(array, pltpu.HBM)


def call(kernel, outs, limit, **options):
    return pl.pallas_call(
        kernel,
        out_shape=outs,
        compiler_params=pltpu.CompilerParams(vmem_limit_bytes=limit),
        **options,
    )


def per_device(pairs, queries, key_vectors, value_vectors, out_grad):
    half_rows, width = queries.shape
    blocks = half_rows // BLOCK
    rows16 = jax.ShapeDtypeStruct((half_rows, width), BF16)
    block32 = jax.ShapeDtypeStruct((BLOCK, width), F32)
    states = jax.ShapeDtypeStruct((2 * width, width), F32)
    halves = jax.ShapeDtypeStruct((2, width // 2, width), F32)
    in_hbm = pl.BlockSpec(memory_space=pltpu.HBM)
    in_vmem = pl.BlockSpec(memory_space=pltpu.VMEM)
    anywhere = pl.BlockSpec(memory_space=pl.ANY)
    send, own, keep, q, k, v, grad = call(
        outer_kernel,
        (halves, halves, states) + (rows16,) * 4,
        2**23,
        in_specs=[in_hbm] * 4,
        scratch_shapes=[
            pltpu.VMEM((half_rows, width), BF16),
            pltpu.VMEM((width, width), F32),
            pltpu.SemaphoreType.DMA((blocks, 4)),
        ],
    )(*(in_memory(x) for x in (queries, key_vectors, value_vectors, out_grad)))

    def in_block(b, *after):
        return call(
            functools.partial(local_kernel, b),
            (block32,) * 4,
            2**24,
            in_specs=[in_vmem] * 4 + [anywhere] * len(after),
            cost_estimate=pl.CostEstimate(
                flops=12 * BLOCK * BLOCK * width, bytes_accessed=2**21, transcendentals=0
            ),
        )(q, k, v, grad, *after)

    got = lax.ppermute(send, AXES, pairs)
    first = in_block(0)
    count = lax.axis_size("seq")
    parts = call(
        spread_kernel,
        jax.ShapeDtypeStruct((count, width // 2, width), F32),
        2**23,
        in_specs=[in_vmem] * 2 + [anywhere],
    )(own, got, first[0])
    parts = lax.all_to_all(parts, "seq", 0, 0)
    send, mine = call(gather_kernel, (halves,) * 2, 2**23)(parts, own, got)
    got = lax.ppermute(send, AXES, pairs)
    second = in_block(1, mine)
    return call(
        final_kernel,
        (rows16,) * 4,
        2**24,
        out_specs=(in_hbm,) * 4,
        scratch_shapes=[pltpu.VMEM((half_rows, width), BF16)] * 4
        + [pltpu.VMEM((2, width, width), F32), pltpu.SemaphoreType.DMA((4 * blocks,))],
    )(q, k, v, grad, mine, got, keep, *first, *second)


def solution(mesh):
    count = mesh.shape["seq"] * mesh.shape["inner"]
    pairs = [(i, i ^ 1) for i in range(count)]
    spec = P("seq", "inner")
    return jax.shard_map(
        functools.partial(per_device, pairs),
        mesh=mesh,
        in_specs=(spec,) * 4,
        out_specs=(spec,) * 4,
        check_vma=False,
    )
```

time: 44.5 us -> 46 us (1.034)
  starting transfers between devices: 3.96 us -> 20.5 us
  waiting for transfers between devices: 7.53 us -> 0.01 us
  blocking collectives: 26.2 us -> 19 us
    ppermute x0 -> x2, starting transfers between devices: none -> 20.5 us  [per_device(): got = lax.ppermute(send, AXES, pairs)]
    all_to_all x1 -> x0, waiting for transfers between devices: 7.53 us -> none  [per_device(): parts = lax.all_to_all(parts, AXES, 0, 0, axis_index_groups=groups)]
    all_to_all x1, blocking collectives: 26.2 us -> 19 us  [per_device(): parts = lax.all_to_all(parts, 'seq', 0, 0)]
    all_to_all x1 -> x0, starting transfers between devices: 3.96 us -> none  [per_device(): parts = lax.all_to_all(parts, AXES, 0, 0, axis_index_groups=groups)]
    pallas_call x3 -> x5, Pallas kernels: 4.66 us -> 4.36 us  [the longest x2 2.16 us: in_block(): call(functools.partial(local_kernel, b), (block32,) * 4, 2 ** 24, in_spec...]
  transfers between devices with their start and end apart: 1 -> 2, of which waited for: 1 -> 0; matrix products, arithmetic and copies ran while one was open for 0% -> 0% of each run, Pallas kernels for 4% -> 5%
where the time goes in v3:
time: 46 us; the launch traced here: 45.8 us
  starting transfers between devices  20.5 us (45%)
  blocking collectives  19 us (41%)
  Pallas kernels  5.66 us (12%)
  between operations  0.69 us (2%)
    ppermute x2, starting transfers between devices, per_device(): got = lax.ppermute(send, AXES, pairs)  20.5 us
    all_to_all x1, blocking collectives, per_device(): parts = lax.all_to_all(parts, 'seq', 0, 0)  19 us
    pallas_call x2, Pallas kernels, in_block(): call(functools.partial(local_kernel, b), (block32,) * 4, 2 ** 24, in_spec...  2.16 us
    pallas_call x1, Pallas kernels, per_device(): call(outer_kernel, (halves, halves, states) + (rows16,) * 4, 2 ** 23, in_...  2.05 us
    pallas_call x1, Pallas kernels, per_device(): call(final_kernel, (rows16,) * 4, 2 ** 24, out_specs=(in_hbm,) * 4, scrat...  1.29 us
  transfers between devices with their start and end apart: 2, of which 0 were waited for; matrix products, arithmetic and copies ran while one was open for 0% of the time, Pallas kernels for 5%

profile of v3, /device:TPU:1, one launch (start us, length us, event | category | flops | bytes accessed | tf_op | source)
XLA Modules:
  0.0 45.8 jit_solution(13342974862648266696)
XLA Ops:
  0.6 2.1 %shard_map.75 = (f32[2,64,128]{2,1,0:T(8,128)S(1)}, f32[2,64,128]{2,1,0:T(8,128)S(1)}, f32[256,128]{1,0:T(8,128)S(1)}, bf16[1024,128]{1,0:T(8,128)(2,1)S(1)}, bf...) custom-call(bf16[1024,128]{1,0:T(8,128)(2,1)} %q_hbm.1, ...), custom_call_target="tpu_custom_call" | custom-call | tf_op jit(solution)/shard_map/pallas_call | solution.py:182
  2.7 16.1 %collective-permute-start = (f32[2,64,128]{2,1,0:T(8,128)S(1)}, f32[2,64,128]{2,1,0:T(8,128)S(1)}, u32[]{:S(2)}, u32[]{:S(2)}) collective-permute-start(f32[2,64,128]{2,1,0:T(8,128)S(1)} %get-tuple-element.26), channel_id=1, source_target_pairs={{0,1},{1,0},{2,3},{3,2},{4,5},{5,4},{6,7},{7,6},{8,9},{9,8},{10,11... | collective-permute-start | bytes 196616 | tf_op jit(solution)/shard_map/ppermute | solution.py:205
  18.8 1.1 %shard_map.76 = (f32[512,128]{1,0:T(8,128)S(1)}, f32[512,128]{1,0:T(8,128)S(1)}, f32[512,128]{1,0:T(8,128)S(1)}, f32[512,128]{1,0:T(8,128)S(1)}) custom-call(bf16[1024,128]{1,0:T(8,128)(2,1)S(1)} %get-tuple-element.21.q_ref, bf16[1024,128]{1,0:T(8,128)(2,1)S(1)} %get-tuple-element.22.k_ref, bf16[1024,128]{1,0:T(8,128)(2,1)S(1)} %get-tuple-element.23.v_ref, ...), custom_call_target="tpu_custom_call" | custom-call | flops 402653184 | bytes 2097152 | tf_op jit(solution)/shard_map/pallas_call | solution.py:195
  19.9 0.0 collective-permute-done.got_ref
  19.9 19.0 %all_to_all.5.parts_ref = f32[16,64,128]{2,1,0:T(8,128)S(1)} all-to-all(f32[16,64,128]{2,1,0:T(8,128)S(1)} %shard_map.77), channel_id=1, replica_groups=mesh['seq'=16,'inner'=64] {'seq'}, dimensions={0} | all-to-all | bytes 1048576 | tf_op jit(solution)/shard_map/all_to_all | solution.py:214
  38.9 0.1 shard_map.78
  39.0 4.4 %collective-permute-start.1 = (f32[2,64,128]{2,1,0:T(8,128)S(1)}, f32[2,64,128]{2,1,0:T(8,128)S(1)}, u32[]{:S(2)}, u32[]{:S(2)}) collective-permute-start(f32[2,64,128]{2,1,0:T(8,128)S(1)} %get-tuple-element.29), channel_id=1, source_target_pairs={{0,1},{1,0},{2,3},{3,2},{4,5},{5,4},{6,7},{7,6},{8,9},{9,8},{10,11... | collective-permute-start | bytes 196616 | tf_op jit(solution)/shard_map/ppermute | solution.py:216
  43.4 1.1 %shard_map.79 = (f32[512,128]{1,0:T(8,128)S(1)}, f32[512,128]{1,0:T(8,128)S(1)}, f32[512,128]{1,0:T(8,128)S(1)}, f32[512,128]{1,0:T(8,128)S(1)}) custom-call(bf16[1024,128]{1,0:T(8,128)(2,1)S(1)} %get-tuple-element.21.q_ref, bf16[1024,128]{1,0:T(8,128)(2,1)S(1)} %get-tuple-element.22.k_ref, bf16[1024,128]{1,0:T(8,128)(2,1)S(1)} %get-tuple-element.23.v_ref, ...), custom_call_target="tpu_custom_call" | custom-call | flops 402653184 | bytes 2097152 | tf_op jit(solution)/shard_map/pallas_call | solution.py:195
  44.5 0.0 collective-permute-done.1.got_ref
  44.5 1.3 %shard_map.80 = (bf16[1024,128]{1,0:T(8,128)(2,1)}, bf16[1024,128]{1,0:T(8,128)(2,1)}, bf16[1024,128]{1,0:T(8,128)(2,1)}, bf16[1024,128]{1,0:T(8,128)(2,1)}) custom-call(bf16[1024,128]{1,0:T(8,128)(2,1)S(1)} %get-tuple-element.21.q_ref, bf16[1024,128]{1,0:T(8,128)(2,1)S(1)} %get-tuple-element.22.k_ref, bf16[1024,128]{1,0:T(8,128)(2,1)S(1)} %get-tuple-element.23.v_ref, ...), custom_call_target="tpu_custom_call" | custom-call | tf_op jit(solution)/shard_map/pallas_call | solution.py:218
  (1 shorter events, 0.0 us)
Async XLA Ops:
  2.7 17.2 %collective-permute-start = (f32[2,64,128]{2,1,0:T(8,128)S(1)}, f32[2,64,128]{2,1,0:T(8,128)S(1)}, u32[]{:S(2)}, u32[]{:S(2)}) collective-permute-start(f32[2,64,128]{2,1,0:T(8,128)S(1)} %get-tuple-element.26), channel_id=1, source_target_pairs={{0,1},{1,0},{2,3},{3,2},{4,5},{5,4},{6,7},{7,6},{8,9},{9,8},{10,11... | collective-permute-start | bytes 196616 | tf_op jit(solution)/shard_map/ppermute | solution.py:205
  39.0 5.5 %collective-permute-start.1 = (f32[2,64,128]{2,1,0:T(8,128)S(1)}, f32[2,64,128]{2,1,0:T(8,128)S(1)}, u32[]{:S(2)}, u32[]{:S(2)}) collective-permute-start(f32[2,64,128]{2,1,0:T(8,128)S(1)} %get-tuple-element.29), channel_id=1, source_target_pairs={{0,1},{1,0},{2,3},{3,2},{4,5},{5,4},{6,7},{7,6},{8,9},{9,8},{10,11... | collective-permute-start | bytes 196616 | tf_op jit(solution)/shard_map/ppermute | solution.py:216

commit v4 on v3

--- a/solution.py
+++ b/solution.py
@@ -60,36 +60,47 @@
     keep_ref[:width, :] = kv[0]
     keep_ref[width:, :] = back[1]
     half = width // 2
-    mine = lax.axis_index("inner") % 2
-    for i, total in enumerate((kv[0] + kv[1], back[0] + back[1])):
-        total_ref[...] = total
-        own_ref[i] = total_ref[pl.ds(mine * half, half), :]
-        send_ref[i] = total_ref[pl.ds((1 - mine) * half, half), :]
+    side = lax.axis_index("inner") % 2
+    total_ref[0] = kv[0] + kv[1]
+    total_ref[1] = back[0] + back[1]
+    own_ref[0] = total_ref[0, pl.ds(side * half, half), :]
+    own_ref[1] = total_ref[1, pl.ds(side * half, half), :]
+    send_ref[:width, :] = total_ref[side]
+    send_ref[width:, :] = total_ref[1 - side, pl.ds((1 - side) * half, half), :]
 
 
 def spread_kernel(own_ref, got_ref, *refs):
     out_ref = refs[-1]
+    count, rows, width = out_ref.shape
+    half = width // 2
     me = lax.axis_index("seq")
-    kv = own_ref[0] + got_ref[0]
-    back = own_ref[1] + got_ref[1]
-    for i in range(out_ref.shape[0]):
-        out_ref[i] = jnp.where(i > me, kv, back)
-
-
-def gather_kernel(parts_ref, own_ref, got_ref, send_ref, mine_ref):
-    me = lax.axis_index("seq")
-    is_second = lax.axis_index("inner") % 2 == 1
+    side = lax.axis_index("inner") % 2
+    whole = got_ref[pl.ds(side * half, half), :]
+    part = got_ref[width:, :]
+    kv = own_ref[0] + jnp.where(side == 0, part, whole)
+    back = own_ref[1] + jnp.where(side == 0, whole, part)
+    for i in range(count):
+        takes_kv = jnp.logical_or(i // 2 > me // 2, (i // 2 == me // 2) & (me % 2 == 0))
+        cut = slice((i % 2) * rows, (i % 2 + 1) * rows)
+        out_ref[i] = jnp.where(takes_kv, kv[cut], back[cut])
+
+
+def gather_kernel(parts_ref, send_ref):
+    pair = lax.axis_index("seq") // 2
     zero = jnp.zeros(parts_ref.shape[1:], F32)
     earlier, later = zero, zero
     count = parts_ref.shape[0]
     for i in range(count):
-        earlier = earlier + jnp.where(i < me, parts_ref[i], zero)
+        earlier = earlier + jnp.where(i // 2 < pair, parts_ref[i], zero)
         j = count - 1 - i
-        later = later + jnp.where(j > me, parts_ref[j], zero)
-    send_ref[0] = earlier + jnp.where(is_second, zero, own_ref[0])
-    send_ref[1] = later + jnp.where(is_second, own_ref[1], zero)
-    mine_ref[0] = earlier + jnp.where(is_second, got_ref[0], zero)
-    mine_ref[1] = later + jnp.where(is_second, zero, got_ref[1])
+        later = later + jnp.where(j // 2 > pair, parts_ref[j], zero)
+    with_first = earlier + parts_ref[2 * pair]
+    with_second = later + parts_ref[2 * pair + 1]
+    for side in range(2):
+        send_ref[side, 0] = earlier
+        send_ref[side, 1] = with_second
+        send_ref[2 + side, 0] = with_first
+        send_ref[2 + side, 1] = later
 
 
 def local_kernel(b, q_ref, k_ref, v_ref, g_ref, *refs):
@@ -119,18 +130,19 @@
             out[pl.ds(i * SUB, SUB), :] = parts[i]
 
 
-def final_kernel(q_ref, k_ref, v_ref, g_ref, mine_ref, got_ref, keep_ref, *refs):
+def final_kernel(q_ref, k_ref, v_ref, g_ref, state_ref, got_ref, keep_ref, *refs):
     local, outs = refs[:8], refs[8:12]
-    buffers, state_ref, sems = refs[12:16], refs[16], refs[17]
+    buffers, sems = refs[12:16], refs[16]
     half_rows, width = q_ref.shape
     start = first_position(half_rows)
-    half = width // 2
-    mine = lax.axis_index("inner") % 2
-    for i in range(2):
-        state_ref[i, pl.ds(mine * half, half), :] = mine_ref[i]
-        state_ref[i, pl.ds((1 - mine) * half, half), :] = got_ref[i]
-    kv0 = state_ref[0]
-    back1 = state_ref[1]
+    is_second = lax.axis_index("inner") % 2 == 1
+    kv0, back1 = (
+        jnp.concatenate([state_ref[2 * z + c, i] for c in range(2) for z in range(2)], 0)
+        for i in range(2)
+    )
+    other = got_ref[:width, :]
+    kv0 = kv0 + jnp.where(is_second, other, 0.0)
+    back1 = back1 + jnp.where(is_second, 0.0, other)
     kv_used = [kv0.astype(BF16), (kv0 + keep_ref[:width, :]).astype(BF16)]
     back_used = [(back1 + keep_ref[width:, :]).astype(BF16), back1.astype(BF16)]
     copies = []
@@ -169,24 +181,26 @@
     )
 
 
-def per_device(pairs, queries, key_vectors, value_vectors, out_grad):
+def per_device(pairs, groups, queries, key_vectors, value_vectors, out_grad):
     half_rows, width = queries.shape
     blocks = half_rows // BLOCK
     rows16 = jax.ShapeDtypeStruct((half_rows, width), BF16)
     block32 = jax.ShapeDtypeStruct((BLOCK, width), F32)
     states = jax.ShapeDtypeStruct((2 * width, width), F32)
-    halves = jax.ShapeDtypeStruct((2, width // 2, width), F32)
+    half = width // 2
+    halves = jax.ShapeDtypeStruct((2, half, width), F32)
+    sent = jax.ShapeDtypeStruct((width + half, width), F32)
     in_hbm = pl.BlockSpec(memory_space=pltpu.HBM)
     in_vmem = pl.BlockSpec(memory_space=pltpu.VMEM)
     anywhere = pl.BlockSpec(memory_space=pl.ANY)
     send, own, keep, q, k, v, grad = call(
         outer_kernel,
-        (halves, halves, states) + (rows16,) * 4,
+        (sent, halves, states) + (rows16,) * 4,
         2**23,
         in_specs=[in_hbm] * 4,
         scratch_shapes=[
             pltpu.VMEM((half_rows, width), BF16),
-            pltpu.VMEM((width, width), F32),
+            pltpu.VMEM((2, width, width), F32),
             pltpu.SemaphoreType.DMA((blocks, 4)),
         ],
     )(*(in_memory(x) for x in (queries, key_vectors, value_vectors, out_grad)))
@@ -205,32 +219,39 @@
     got = lax.ppermute(send, AXES, pairs)
     first = in_block(0)
     count = lax.axis_size("seq")
+    quarter = half // 2
     parts = call(
         spread_kernel,
-        jax.ShapeDtypeStruct((count, width // 2, width), F32),
+        jax.ShapeDtypeStruct((count, quarter, width), F32),
         2**23,
         in_specs=[in_vmem] * 2 + [anywhere],
     )(own, got, first[0])
     parts = lax.all_to_all(parts, "seq", 0, 0)
-    send, mine = call(gather_kernel, (halves,) * 2, 2**23)(parts, own, got)
-    got = lax.ppermute(send, AXES, pairs)
-    second = in_block(1, mine)
+    quads = jax.ShapeDtypeStruct((4, 2, quarter, width), F32)
+    state = call(gather_kernel, quads, 2**23)(parts)
+    second = in_block(1, state)
+    state = lax.all_to_all(state, AXES, 0, 0, axis_index_groups=groups)
     return call(
         final_kernel,
         (rows16,) * 4,
         2**24,
         out_specs=(in_hbm,) * 4,
         scratch_shapes=[pltpu.VMEM((half_rows, width), BF16)] * 4
-        + [pltpu.VMEM((2, width, width), F32), pltpu.SemaphoreType.DMA((4 * blocks,))],
-    )(q, k, v, grad, mine, got, keep, *first, *second)
+        + [pltpu.SemaphoreType.DMA((4 * blocks,))],
+    )(q, k, v, grad, state, got, keep, *first, *second)
 
 
 def solution(mesh):
-    count = mesh.shape["seq"] * mesh.shape["inner"]
-    pairs = [(i, i ^ 1) for i in range(count)]
+    n_seq, n_inner = mesh.shape["seq"], mesh.shape["inner"]
+    pairs = [(i, i ^ 1) for i in range(n_seq * n_inner)]
+    groups = [
+        [(2 * x + z) * n_inner + 2 * h + side for z in range(2) for side in range(2)]
+        for x in range(n_seq // 2)
+        for h in range(n_inner // 2)
+    ]
     spec = P("seq", "inner")
     return jax.shard_map(
-        functools.partial(per_device, pairs),
+        functools.partial(per_device, pairs, groups),
         mesh=mesh,
         in_specs=(spec,) * 4,
         out_specs=(spec,) * 4,

time: 46 us -> 45.1 us (0.980)
  blocking collectives: 19 us -> 14.1 us
  waiting for transfers between devices: 0.01 us -> 2.51 us
  starting transfers between devices: 20.5 us -> 21.3 us
  Pallas kernels: 5.66 us -> 6.25 us
    all_to_all x0 -> x1, starting transfers between devices: none -> 5.21 us  [per_device(): state = lax.all_to_all(state, AXES, 0, 0, axis_index_groups=groups)]
    all_to_all x1, blocking collectives: 19 us -> 14.1 us  [per_device(): parts = lax.all_to_all(parts, 'seq', 0, 0)]
    ppermute x2 -> x1, starting transfers between devices: 20.5 us -> 16.1 us  [per_device(): got = lax.ppermute(send, AXES, pairs)]
    all_to_all x0 -> x1, waiting for transfers between devices: none -> 2.51 us  [per_device(): state = lax.all_to_all(state, AXES, 0, 0, axis_index_groups=groups)]
    pallas_call x3, Pallas kernels: 2.2 us -> 2.81 us  [the longest x1 2.06 us: per_device(): call(outer_kernel, (sent, halves, states) + (rows16,) * 4, 2 ** 23, in_sp...]
  transfers between devices with their start and end apart: 2 -> 2, of which waited for: 0 -> 1; matrix products, arithmetic and copies ran while one was open for 0% -> 0% of each run, Pallas kernels for 5% -> 5%
where the time goes in v4:
time: 45.1 us; the launch traced here: 44.8 us
  starting transfers between devices  21.3 us (47%)
  blocking collectives  14.1 us (31%)
  Pallas kernels  6.25 us (14%)
  waiting for transfers between devices  2.51 us (6%)
  between operations  0.67 us (1%)
    ppermute x1, starting transfers between devices, per_device(): got = lax.ppermute(send, AXES, pairs)  16.1 us
    all_to_all x1, blocking collectives, per_device(): parts = lax.all_to_all(parts, 'seq', 0, 0)  14.1 us
    all_to_all x1, starting transfers between devices, per_device(): state = lax.all_to_all(state, AXES, 0, 0, axis_index_groups=groups)  5.21 us
    all_to_all x1, waiting for transfers between devices, per_device(): state = lax.all_to_all(state, AXES, 0, 0, axis_index_groups=groups)  2.51 us
    pallas_call x2, Pallas kernels, in_block(): call(functools.partial(local_kernel, b), (block32,) * 4, 2 ** 24, in_spec...  2.16 us
    pallas_call x1, Pallas kernels, per_device(): call(outer_kernel, (sent, halves, states) + (rows16,) * 4, 2 ** 23, in_sp...  2.06 us
    pallas_call x1, Pallas kernels, per_device(): call(final_kernel, (rows16,) * 4, 2 ** 24, out_specs=(in_hbm,) * 4, scrat...  1.27 us
  transfers between devices with their start and end apart: 2, of which 1 were waited for; matrix products, arithmetic and copies ran while one was open for 0% of the time, Pallas kernels for 5%

profile of v4, /device:TPU:1, one launch (start us, length us, event | category | flops | bytes accessed | tf_op | source)
XLA Modules:
  0.0 44.8 jit_solution(5295079265305982927)
XLA Ops:
  0.6 2.1 %shard_map.75 = (f32[192,128]{1,0:T(8,128)S(1)}, f32[2,64,128]{2,1,0:T(8,128)S(1)}, f32[256,128]{1,0:T(8,128)S(1)}, bf16[1024,128]{1,0:T(8,128)(2,1)S(1)}, bf16[...) custom-call(bf16[1024,128]{1,0:T(8,128)(2,1)} %q_hbm.1, ...), custom_call_target="tpu_custom_call" | custom-call | tf_op jit(solution)/shard_map/pallas_call | solution.py:196
  2.7 16.1 %collective-permute-start = (f32[192,128]{1,0:T(8,128)S(1)}, f32[192,128]{1,0:T(8,128)S(1)}, u32[]{:S(2)}, u32[]{:S(2)}) collective-permute-start(f32[192,128]{1,0:T(8,128)S(1)} %get-tuple-element.24), channel_id=1, source_target_pairs={{0,1},{1,0},{2,3},{3,2},{4,5},{5,4},{6,7},{7,6},{8,9},{9,8},{10,11... | collective-permute-start | bytes 294920 | tf_op jit(solution)/shard_map/ppermute | solution.py:219
  18.8 1.1 %shard_map.76 = (f32[512,128]{1,0:T(8,128)S(1)}, f32[512,128]{1,0:T(8,128)S(1)}, f32[512,128]{1,0:T(8,128)S(1)}, f32[512,128]{1,0:T(8,128)S(1)}) custom-call(bf16[1024,128]{1,0:T(8,128)(2,1)S(1)} %get-tuple-element.19.q_ref, bf16[1024,128]{1,0:T(8,128)(2,1)S(1)} %get-tuple-element.20.k_ref, bf16[1024,128]{1,0:T(8,128)(2,1)S(1)} %get-tuple-element.21.v_ref, ...), custom_call_target="tpu_custom_call" | custom-call | flops 402653184 | bytes 2097152 | tf_op jit(solution)/shard_map/pallas_call | solution.py:209
  19.8 0.0 collective-permute-done.got_ref
  19.9 14.1 %all_to_all.10.parts_ref = f32[16,32,128]{2,1,0:T(8,128)S(1)} all-to-all(f32[16,32,128]{2,1,0:T(8,128)S(1)} %shard_map.77), channel_id=1, replica_groups=mesh['seq'=16,'inner'=64] {'seq'}, dimensions={0} | all-to-all | bytes 524288 | tf_op jit(solution)/shard_map/all_to_all | solution.py:229
  34.0 0.7 %shard_map.78.refs_0_ = f32[4,2,32,128]{3,2,1,0:T(8,128)} custom-call(f32[16,32,128]{2,1,0:T(8,128)S(1)} %all_to_all.10.parts_ref), custom_call_target="tpu_custom_call" | custom-call | tf_op jit(solution)/shard_map/pallas_call | solution.py:231
  34.7 5.2 %all-to-all-start.1 = ((f32[4,2,32,128]{3,2,1,0:T(8,128)}), f32[4,2,32,128]{3,2,1,0:T(8,128)S(1)}, u32[]{:S(2)}, u32[]{:S(2)}) async-start(f32[4,2,32,128]{3,2,1,0:T(8,128)} %shard_map.78.refs_0_), calls=%async_computation.1 | async-start | bytes 262144 | tf_op jit(solution)/shard_map/all_to_all | solution.py:233
  39.9 1.1 %shard_map.79 = (f32[512,128]{1,0:T(8,128)S(1)}, f32[512,128]{1,0:T(8,128)S(1)}, f32[512,128]{1,0:T(8,128)S(1)}, f32[512,128]{1,0:T(8,128)S(1)}) custom-call(bf16[1024,128]{1,0:T(8,128)(2,1)S(1)} %get-tuple-element.19.q_ref, bf16[1024,128]{1,0:T(8,128)(2,1)S(1)} %get-tuple-element.20.k_ref, bf16[1024,128]{1,0:T(8,128)(2,1)S(1)} %get-tuple-element.21.v_ref, ...), custom_call_target="tpu_custom_call" | custom-call | flops 402653184 | bytes 2097152 | tf_op jit(solution)/shard_map/pallas_call | solution.py:209
  41.0 2.5 %all-to-all-done.1.state_ref = f32[4,2,32,128]{3,2,1,0:T(8,128)S(1)} async-done(((f32[4,2,32,128]{3,2,1,0:T(8,128)}), f32[4,2,32,128]{3,2,1,0:T(8,128)S(1)}, u32[]{:S(2)}, u32[]{:S(2)}) %all-to-all-start.1) | async-done | bytes 131104 | tf_op jit(solution)/shard_map/all_to_all | solution.py:233
  43.5 1.3 %shard_map.80 = (bf16[1024,128]{1,0:T(8,128)(2,1)}, bf16[1024,128]{1,0:T(8,128)(2,1)}, bf16[1024,128]{1,0:T(8,128)(2,1)}, bf16[1024,128]{1,0:T(8,128)(2,1)}) custom-call(bf16[1024,128]{1,0:T(8,128)(2,1)S(1)} %get-tuple-element.19.q_ref, bf16[1024,128]{1,0:T(8,128)(2,1)S(1)} %get-tuple-element.20.k_ref, bf16[1024,128]{1,0:T(8,128)(2,1)S(1)} %get-tuple-element.21.v_ref, ...), custom_call_target="tpu_custom_call" | custom-call | tf_op jit(solution)/shard_map/pallas_call | solution.py:234
  (1 shorter events, 0.0 us)
Async XLA Ops:
  2.7 17.1 %collective-permute-start = (f32[192,128]{1,0:T(8,128)S(1)}, f32[192,128]{1,0:T(8,128)S(1)}, u32[]{:S(2)}, u32[]{:S(2)}) collective-permute-start(f32[192,128]{1,0:T(8,128)S(1)} %get-tuple-element.24), channel_id=1, source_target_pairs={{0,1},{1,0},{2,3},{3,2},{4,5},{5,4},{6,7},{7,6},{8,9},{9,8},{10,11... | collective-permute-start | bytes 294920 | tf_op jit(solution)/shard_map/ppermute | solution.py:219
  34.7 8.8 %all-to-all-start.1 = ((f32[4,2,32,128]{3,2,1,0:T(8,128)}), f32[4,2,32,128]{3,2,1,0:T(8,128)S(1)}, u32[]{:S(2)}, u32[]{:S(2)}) async-start(f32[4,2,32,128]{3,2,1,0:T(8,128)} %shard_map.78.refs_0_), calls=%async_computation.1 | async-start | bytes 262144 | tf_op jit(solution)/shard_map/all_to_all | solution.py:233

commit v5 on v4

--- a/solution.py
+++ b/solution.py
@@ -103,36 +103,41 @@
         send_ref[2 + side, 1] = later
 
 
-def local_kernel(b, q_ref, k_ref, v_ref, g_ref, *refs):
-    outs = refs[-4:]
+def local_kernel(q_ref, k_ref, v_ref, g_ref, att_ref, qg_ref, kg_ref, vg_ref):
     row = lax.broadcasted_iota(jnp.int32, (SUB, SUB), 0)
     col = lax.broadcasted_iota(jnp.int32, (SUB, SUB), 1)
     causal = row >= col
     n = BLOCK // SUB
-    tiles = [pl.ds(b * BLOCK + i * SUB, SUB) for i in range(n)]
-    q, k, v, g = ([ref[t, :] for t in tiles] for ref in (q_ref, k_ref, v_ref, g_ref))
-    att, qg, kg, vg = ([0.0] * n for _ in range(4))
-    for i in range(n):
-        for j in range(i + 1):
-            w = dot(q[i], k[j], 1, 1)
-            s = dot(g[i], v[j], 1, 1)
-            if i == j:
-                w = jnp.where(causal, w, 0.0)
-                s = jnp.where(causal, s, 0.0)
-            w = w.astype(BF16)
-            s = s.astype(BF16)
-            att[i] = att[i] + dot(w, v[j], 1, 0)
-            qg[i] = qg[i] + dot(s, k[j], 1, 0)
-            kg[j] = kg[j] + dot(s, q[i], 0, 0)
-            vg[j] = vg[j] + dot(w, g[i], 0, 0)
-    for out, parts in zip(outs, (att, qg, kg, vg)):
+
+    def masked(scores):
+        left = scores.shape[1] - SUB
+        last = jnp.where(causal, scores[:, left:], 0.0)
+        if left:
+            last = jnp.concatenate([scores[:, :left], last], 1)
+        return last.astype(BF16)
+
+    for b in range(q_ref.shape[0] // BLOCK):
+        weights, scores = [], []
         for i in range(n):
-            out[pl.ds(i * SUB, SUB), :] = parts[i]
+            own = pl.ds(b * BLOCK + i * SUB, SUB)
+            before = pl.ds(b * BLOCK, (i + 1) * SUB)
+            weights.append(masked(dot(q_ref[own, :], k_ref[before, :], 1, 1)))
+            scores.append(masked(dot(g_ref[own, :], v_ref[before, :], 1, 1)))
+            att_ref[own, :] = dot(weights[i], v_ref[before, :], 1, 0)
+            qg_ref[own, :] = dot(scores[i], k_ref[before, :], 1, 0)
+        for j in range(n):
+            own = pl.ds(b * BLOCK + j * SUB, SUB)
+            after = pl.ds(b * BLOCK + j * SUB, (n - j) * SUB)
+            cut = slice(j * SUB, (j + 1) * SUB)
+            w = jnp.concatenate([weights[i][:, cut] for i in range(j, n)], 0)
+            s = jnp.concatenate([scores[i][:, cut] for i in range(j, n)], 0)
+            vg_ref[own, :] = dot(w, g_ref[after, :], 0, 0)
+            kg_ref[own, :] = dot(s, q_ref[after, :], 0, 0)
 
 
 def final_kernel(q_ref, k_ref, v_ref, g_ref, state_ref, got_ref, keep_ref, *refs):
-    local, outs = refs[:8], refs[8:12]
-    buffers, sems = refs[12:16], refs[16]
+    local, outs = refs[:4], refs[4:8]
+    buffers, sems = refs[8:12], refs[12]
     half_rows, width = q_ref.shape
     start = first_position(half_rows)
     is_second = lax.axis_index("inner") % 2 == 1
@@ -158,7 +163,7 @@
     for b in range(half_rows // BLOCK):
         rows = pl.ds(b * BLOCK, BLOCK)
         q, k, v, g = q_ref[rows, :], k_ref[rows, :], v_ref[rows, :], g_ref[rows, :]
-        att, qg, kg, vg = (ref[...] for ref in local[4 * b : 4 * b + 4])
+        att, qg, kg, vg = (ref[rows, :] for ref in local)
         put(1, qg + dot(g, kv_used[b], 1, 1), rows)
         put(2, kg + dot(v, back_used[b], 1, 1), rows)
         put(3, vg + dot(k, back_used[b], 1, 0), rows)
@@ -185,7 +190,7 @@
     half_rows, width = queries.shape
     blocks = half_rows // BLOCK
     rows16 = jax.ShapeDtypeStruct((half_rows, width), BF16)
-    block32 = jax.ShapeDtypeStruct((BLOCK, width), F32)
+    rows32 = jax.ShapeDtypeStruct((half_rows, width), F32)
     states = jax.ShapeDtypeStruct((2 * width, width), F32)
     half = width // 2
     halves = jax.ShapeDtypeStruct((2, half, width), F32)
@@ -205,19 +210,15 @@
         ],
     )(*(in_memory(x) for x in (queries, key_vectors, value_vectors, out_grad)))
 
-    def in_block(b, *after):
-        return call(
-            functools.partial(local_kernel, b),
-            (block32,) * 4,
-            2**24,
-            in_specs=[in_vmem] * 4 + [anywhere] * len(after),
-            cost_estimate=pl.CostEstimate(
-                flops=12 * BLOCK * BLOCK * width, bytes_accessed=2**21, transcendentals=0
-            ),
-        )(q, k, v, grad, *after)
-
     got = lax.ppermute(send, AXES, pairs)
-    first = in_block(0)
+    local = call(
+        local_kernel,
+        (rows32,) * 4,
+        2**24,
+        cost_estimate=pl.CostEstimate(
+            flops=12 * half_rows * BLOCK * width, bytes_accessed=2**22, transcendentals=0
+        ),
+    )(q, k, v, grad)
     count = lax.axis_size("seq")
     quarter = half // 2
     parts = call(
@@ -225,11 +226,10 @@
         jax.ShapeDtypeStruct((count, quarter, width), F32),
         2**23,
         in_specs=[in_vmem] * 2 + [anywhere],
-    )(own, got, first[0])
+    )(own, got, local[0])
     parts = lax.all_to_all(parts, "seq", 0, 0)
     quads = jax.ShapeDtypeStruct((4, 2, quarter, width), F32)
     state = call(gather_kernel, quads, 2**23)(parts)
-    second = in_block(1, state)
     state = lax.all_to_all(state, AXES, 0, 0, axis_index_groups=groups)
     return call(
         final_kernel,
@@ -238,7 +238,7 @@
         out_specs=(in_hbm,) * 4,
         scratch_shapes=[pltpu.VMEM((half_rows, width), BF16)] * 4
         + [pltpu.SemaphoreType.DMA((4 * blocks,))],
-    )(q, k, v, grad, state, got, keep, *first, *second)
+    )(q, k, v, grad, state, got, keep, *local)
 
 
 def solution(mesh):

time: 45.1 us -> 43.9 us (0.973)
  blocking collectives: 14.1 us -> 22 us
  starting transfers between devices: 21.3 us -> 16.1 us
  waiting for transfers between devices: 2.51 us -> 0.01 us
  Pallas kernels: 6.25 us -> 4.97 us
    all_to_all x0 -> x1, blocking collectives: none -> 7.8 us  [per_device(): state = lax.all_to_all(state, AXES, 0, 0, axis_index_groups=groups)]
    all_to_all x1 -> x0, starting transfers between devices: 5.21 us -> none  [per_device(): state = lax.all_to_all(state, AXES, 0, 0, axis_index_groups=groups)]
    all_to_all x1 -> x0, waiting for transfers between devices: 2.51 us -> none  [per_device(): state = lax.all_to_all(state, AXES, 0, 0, axis_index_groups=groups)]
    pallas_call x1, Pallas kernels: 0.71 us -> 0.06 us  [per_device(): state = call(gather_kernel, quads, 2 ** 23)(parts)]
    pallas_call x2 -> x1, Pallas kernels: 2.16 us -> 1.53 us  [per_device(): call(local_kernel, (rows32,) * 4, 2 ** 24, cost_estimate=pl.CostEstimate(...]
  transfers between devices with their start and end apart: 2 -> 1, of which waited for: 1 -> 0; matrix products, arithmetic and copies ran while one was open for 0% -> 0% of each run, Pallas kernels for 5% -> 4%
where the time goes in v5:
time: 43.9 us; the launch traced here: 43.7 us
  blocking collectives  22 us (50%)
  starting transfers between devices  16.1 us (37%)
  Pallas kernels  4.97 us (11%)
  between operations  0.68 us (2%)
    ppermute x1, starting transfers between devices, per_device(): got = lax.ppermute(send, AXES, pairs)  16.1 us
    all_to_all x1, blocking collectives, per_device(): parts = lax.all_to_all(parts, 'seq', 0, 0)  14.2 us
    all_to_all x1, blocking collectives, per_device(): state = lax.all_to_all(state, AXES, 0, 0, axis_index_groups=groups)  7.8 us
    pallas_call x1, Pallas kernels, per_device(): call(outer_kernel, (sent, halves, states) + (rows16,) * 4, 2 ** 23, in_sp...  2.06 us
    pallas_call x1, Pallas kernels, per_device(): call(local_kernel, (rows32,) * 4, 2 ** 24, cost_estimate=pl.CostEstimate(...  1.53 us
    pallas_call x1, Pallas kernels, per_device(): call(final_kernel, (rows16,) * 4, 2 ** 24, out_specs=(in_hbm,) * 4, scrat...  1.27 us
  transfers between devices with their start and end apart: 1, of which 0 were waited for; matrix products, arithmetic and copies ran while one was open for 0% of the time, Pallas kernels for 4%

profile of v5, /device:TPU:1, one launch (start us, length us, event | category | flops | bytes accessed | tf_op | source)
XLA Modules:
  0.0 43.7 jit_solution(361459684617287376)
XLA Ops:
  0.6 2.1 %shard_map.75 = (f32[192,128]{1,0:T(8,128)S(1)}, f32[2,64,128]{2,1,0:T(8,128)S(1)}, f32[256,128]{1,0:T(8,128)S(1)}, bf16[1024,128]{1,0:T(8,128)(2,1)S(1)}, bf16[...) custom-call(bf16[1024,128]{1,0:T(8,128)(2,1)} %q_hbm.1, ...), custom_call_target="tpu_custom_call" | custom-call | tf_op jit(solution)/shard_map/pallas_call | solution.py:201
  2.7 16.1 %collective-permute-start = (f32[192,128]{1,0:T(8,128)S(1)}, f32[192,128]{1,0:T(8,128)S(1)}, u32[]{:S(2)}, u32[]{:S(2)}) collective-permute-start(f32[192,128]{1,0:T(8,128)S(1)} %get-tuple-element.20), channel_id=1, source_target_pairs={{0,1},{1,0},{2,3},{3,2},{4,5},{5,4},{6,7},{7,6},{8,9},{9,8},{10,11... | collective-permute-start | bytes 294920 | tf_op jit(solution)/shard_map/ppermute | solution.py:213
  18.8 1.5 %shard_map.76 = (f32[1024,128]{1,0:T(8,128)S(1)}, f32[1024,128]{1,0:T(8,128)S(1)}, f32[1024,128]{1,0:T(8,128)S(1)}, f32[1024,128]{1,0:T(8,128)S(1)}) custom-call(bf16[1024,128]{1,0:T(8,128)(2,1)S(1)} %get-tuple-element.15.q_ref, bf16[1024,128]{1,0:T(8,128)(2,1)S(1)} %get-tuple-element.16.k_ref, bf16[1024,128]{1,0:T(8,128)(2,1)S(1)} %get-tuple-element.17.v_ref, ...), custom_call_target="tpu_custom_call" | custom-call | flops 805306368 | bytes 4194304 | tf_op jit(solution)/shard_map/pallas_call | solution.py:214
  20.3 0.0 collective-permute-done.got_ref
  20.4 14.2 %all_to_all.10.parts_ref = f32[16,32,128]{2,1,0:T(8,128)S(1)} all-to-all(f32[16,32,128]{2,1,0:T(8,128)S(1)} %shard_map.77), channel_id=1, replica_groups=mesh['seq'=16,'inner'=64] {'seq'}, dimensions={0} | all-to-all | bytes 524288 | tf_op jit(solution)/shard_map/all_to_all | solution.py:230
  34.6 0.1 shard_map.78
  34.6 7.8 %all_to_all.11.state_ref = f32[4,2,32,128]{3,2,1,0:T(8,128)S(1)} all-to-all(f32[4,2,32,128]{3,2,1,0:T(8,128)S(1)} %shard_map.78), channel_id=1, replica_groups={{0,1,64,65},{2,3,66,67},{4,5,68,69},{6,7,70,71},{8,9,72,73},{10,11,74,7..., dimensions={0} | all-to-all | bytes 262144 | tf_op jit(solution)/shard_map/all_to_all | solution.py:233
  42.4 1.3 %shard_map.79 = (bf16[1024,128]{1,0:T(8,128)(2,1)}, bf16[1024,128]{1,0:T(8,128)(2,1)}, bf16[1024,128]{1,0:T(8,128)(2,1)}, bf16[1024,128]{1,0:T(8,128)(2,1)}) custom-call(bf16[1024,128]{1,0:T(8,128)(2,1)S(1)} %get-tuple-element.15.q_ref, bf16[1024,128]{1,0:T(8,128)(2,1)S(1)} %get-tuple-element.16.k_ref, bf16[1024,128]{1,0:T(8,128)(2,1)S(1)} %get-tuple-element.17.v_ref, ...), custom_call_target="tpu_custom_call" | custom-call | tf_op jit(solution)/shard_map/pallas_call | solution.py:234
  (1 shorter events, 0.0 us)
Async XLA Ops:
  2.7 17.6 %collective-permute-start = (f32[192,128]{1,0:T(8,128)S(1)}, f32[192,128]{1,0:T(8,128)S(1)}, u32[]{:S(2)}, u32[]{:S(2)}) collective-permute-start(f32[192,128]{1,0:T(8,128)S(1)} %get-tuple-element.20), channel_id=1, source_target_pairs={{0,1},{1,0},{2,3},{3,2},{4,5},{5,4},{6,7},{7,6},{8,9},{9,8},{10,11... | collective-permute-start | bytes 294920 | tf_op jit(solution)/shard_map/ppermute | solution.py:213

commit v6 on v5

--- a/solution.py
+++ b/solution.py
@@ -21,7 +21,7 @@
 def scaling_of(start, rows, width):
     row = lax.broadcasted_iota(jnp.int32, (rows, width), 0)
     position = (start + row).astype(F32)
-    return 1.0 / jnp.sqrt(width * (position + 1.0))
+    return lax.rsqrt(width * (position + 1.0))
 
 
 def first_position(half_rows):
@@ -30,32 +30,27 @@
 
 def outer_kernel(
     q_hbm, k_hbm, v_hbm, o_hbm,
-    send_ref, own_ref, keep_ref, q_ref, k_ref, v_ref, grad_ref,
+    send_ref, own_ref, keep_ref, q_ref, k_ref, v_ref, grad_ref, scale_ref,
     o_ref, total_ref, sems,
 ):
     half_rows, width = q_ref.shape
     start = first_position(half_rows)
     pairs = ((k_hbm, k_ref), (v_hbm, v_ref), (o_hbm, o_ref), (q_hbm, q_ref))
-    copies = []
-    for b in range(half_rows // BLOCK):
-        rows = pl.ds(b * BLOCK, BLOCK)
-        for i, (source, target) in enumerate(pairs):
-            copies.append(
-                pltpu.make_async_copy(source.at[rows, :], target.at[rows, :], sems.at[b, i])
-            )
+    copies = [
+        pltpu.make_async_copy(source, target, sems.at[i])
+        for i, (source, target) in enumerate(pairs)
+    ]
     for copy in copies:
         copy.start()
+    scale_ref[...] = scaling_of(start, half_rows, width)
+    for copy in copies:
+        copy.wait()
     kv, back = [], []
     for b in range(half_rows // BLOCK):
         rows = pl.ds(b * BLOCK, BLOCK)
-        scaling = scaling_of(start + b * BLOCK, BLOCK, width)
-        copies[4 * b].wait()
-        copies[4 * b + 1].wait()
+        grad = (scale_ref[rows, :] * o_ref[rows, :].astype(F32)).astype(BF16)
+        grad_ref[rows, :] = grad
         kv.append(dot(k_ref[rows, :], v_ref[rows, :], 0, 0))
-        copies[4 * b + 2].wait()
-        grad = (scaling * o_ref[rows, :].astype(F32)).astype(BF16)
-        grad_ref[rows, :] = grad
-        copies[4 * b + 3].wait()
         back.append(dot(q_ref[rows, :], grad, 0, 0))
     keep_ref[:width, :] = kv[0]
     keep_ref[width:, :] = back[1]
@@ -135,11 +130,12 @@
             kg_ref[own, :] = dot(s, q_ref[after, :], 0, 0)
 
 
-def final_kernel(q_ref, k_ref, v_ref, g_ref, state_ref, got_ref, keep_ref, *refs):
+def final_kernel(
+    q_ref, k_ref, v_ref, g_ref, scale_ref, state_ref, got_ref, keep_ref, *refs
+):
     local, outs = refs[:4], refs[4:8]
     buffers, sems = refs[8:12], refs[12]
     half_rows, width = q_ref.shape
-    start = first_position(half_rows)
     is_second = lax.axis_index("inner") % 2 == 1
     kv0, back1 = (
         jnp.concatenate([state_ref[2 * z + c, i] for c in range(2) for z in range(2)], 0)
@@ -167,8 +163,7 @@
         put(1, qg + dot(g, kv_used[b], 1, 1), rows)
         put(2, kg + dot(v, back_used[b], 1, 1), rows)
         put(3, vg + dot(k, back_used[b], 1, 0), rows)
-        scaling = scaling_of(start + b * BLOCK, BLOCK, width)
-        put(0, (att + dot(q, kv_used[b], 1, 0)) * scaling, rows)
+        put(0, (att + dot(q, kv_used[b], 1, 0)) * scale_ref[rows, :], rows)
     for copy in copies:
         copy.wait()
 
@@ -198,15 +193,15 @@
     in_hbm = pl.BlockSpec(memory_space=pltpu.HBM)
     in_vmem = pl.BlockSpec(memory_space=pltpu.VMEM)
     anywhere = pl.BlockSpec(memory_space=pl.ANY)
-    send, own, keep, q, k, v, grad = call(
+    send, own, keep, q, k, v, grad, scale = call(
         outer_kernel,
-        (sent, halves, states) + (rows16,) * 4,
+        (sent, halves, states) + (rows16,) * 4 + (rows32,),
         2**23,
         in_specs=[in_hbm] * 4,
         scratch_shapes=[
             pltpu.VMEM((half_rows, width), BF16),
             pltpu.VMEM((2, width, width), F32),
-            pltpu.SemaphoreType.DMA((blocks, 4)),
+            pltpu.SemaphoreType.DMA((4,)),
         ],
     )(*(in_memory(x) for x in (queries, key_vectors, value_vectors, out_grad)))
 
@@ -238,7 +233,7 @@
         out_specs=(in_hbm,) * 4,
         scratch_shapes=[pltpu.VMEM((half_rows, width), BF16)] * 4
         + [pltpu.SemaphoreType.DMA((4 * blocks,))],
-    )(q, k, v, grad, state, got, keep, *local)
+    )(q, k, v, grad, scale, state, got, keep, *local)
 
 
 def solution(mesh):

time: 43.9 us -> 43.5 us (level)
  Pallas kernels: 4.97 us -> 4.49 us
    pallas_call x1, Pallas kernels: 2.06 us -> 1.59 us  [per_device(): call(outer_kernel, (sent, halves, states) + (rows16,) * 4 + (rows32,), 2...]
where the time goes in v6:
time: 43.5 us; the launch traced here: 43.2 us
  blocking collectives  22 us (51%)
  starting transfers between devices  16.1 us (37%)
  Pallas kernels  4.49 us (10%)
  between operations  0.68 us (2%)
    ppermute x1, starting transfers between devices, per_device(): got = lax.ppermute(send, AXES, pairs)  16.1 us
    all_to_all x1, blocking collectives, per_device(): parts = lax.all_to_all(parts, 'seq', 0, 0)  14.2 us
    all_to_all x1, blocking collectives, per_device(): state = lax.all_to_all(state, AXES, 0, 0, axis_index_groups=groups)  7.8 us
    pallas_call x1, Pallas kernels, per_device(): call(outer_kernel, (sent, halves, states) + (rows16,) * 4 + (rows32,), 2...  1.59 us
    pallas_call x1, Pallas kernels, per_device(): call(local_kernel, (rows32,) * 4, 2 ** 24, cost_estimate=pl.CostEstimate(...  1.53 us
    pallas_call x1, Pallas kernels, per_device(): call(final_kernel, (rows16,) * 4, 2 ** 24, out_specs=(in_hbm,) * 4, scrat...  1.27 us
  transfers between devices with their start and end apart: 1, of which 0 were waited for; matrix products, arithmetic and copies ran while one was open for 0% of the time, Pallas kernels for 4%

profile of v6, /device:TPU:1, one launch (start us, length us, event | category | flops | bytes accessed | tf_op | source)
XLA Modules:
  0.0 43.2 jit_solution(13299068519521934666)
XLA Ops:
  0.6 1.6 %shard_map.75 = (f32[192,128]{1,0:T(8,128)S(1)}, f32[2,64,128]{2,1,0:T(8,128)S(1)}, f32[256,128]{1,0:T(8,128)S(1)}, bf16[1024,128]{1,0:T(8,128)(2,1)S(1)}, bf16[...) custom-call(bf16[1024,128]{1,0:T(8,128)(2,1)} %q_hbm.1, ...), custom_call_target="tpu_custom_call" | custom-call | tf_op jit(solution)/shard_map/pallas_call | solution.py:196
  2.2 16.1 %collective-permute-start = (f32[192,128]{1,0:T(8,128)S(1)}, f32[192,128]{1,0:T(8,128)S(1)}, u32[]{:S(2)}, u32[]{:S(2)}) collective-permute-start(f32[192,128]{1,0:T(8,128)S(1)} %get-tuple-element.22), channel_id=1, source_target_pairs={{0,1},{1,0},{2,3},{3,2},{4,5},{5,4},{6,7},{7,6},{8,9},{9,8},{10,11... | collective-permute-start | bytes 294920 | tf_op jit(solution)/shard_map/ppermute | solution.py:208
  18.3 1.5 %shard_map.76 = (f32[1024,128]{1,0:T(8,128)S(1)}, f32[1024,128]{1,0:T(8,128)S(1)}, f32[1024,128]{1,0:T(8,128)S(1)}, f32[1024,128]{1,0:T(8,128)S(1)}) custom-call(bf16[1024,128]{1,0:T(8,128)(2,1)S(1)} %get-tuple-element.16.q_ref, bf16[1024,128]{1,0:T(8,128)(2,1)S(1)} %get-tuple-element.17.k_ref, bf16[1024,128]{1,0:T(8,128)(2,1)S(1)} %get-tuple-element.18.v_ref, ...), custom_call_target="tpu_custom_call" | custom-call | flops 805306368 | bytes 4194304 | tf_op jit(solution)/shard_map/pallas_call | solution.py:209
  19.8 0.0 collective-permute-done.got_ref
  19.9 14.2 %all_to_all.10.parts_ref = f32[16,32,128]{2,1,0:T(8,128)S(1)} all-to-all(f32[16,32,128]{2,1,0:T(8,128)S(1)} %shard_map.77), channel_id=1, replica_groups=mesh['seq'=16,'inner'=64] {'seq'}, dimensions={0} | all-to-all | bytes 524288 | tf_op jit(solution)/shard_map/all_to_all | solution.py:225
  34.1 0.1 shard_map.78
  34.2 7.8 %all_to_all.11.state_ref = f32[4,2,32,128]{3,2,1,0:T(8,128)S(1)} all-to-all(f32[4,2,32,128]{3,2,1,0:T(8,128)S(1)} %shard_map.78), channel_id=1, replica_groups={{0,1,64,65},{2,3,66,67},{4,5,68,69},{6,7,70,71},{8,9,72,73},{10,11,74,7..., dimensions={0} | all-to-all | bytes 262144 | tf_op jit(solution)/shard_map/all_to_all | solution.py:228
  42.0 1.3 %shard_map.79 = (bf16[1024,128]{1,0:T(8,128)(2,1)}, bf16[1024,128]{1,0:T(8,128)(2,1)}, bf16[1024,128]{1,0:T(8,128)(2,1)}, bf16[1024,128]{1,0:T(8,128)(2,1)}) custom-call(bf16[1024,128]{1,0:T(8,128)(2,1)S(1)} %get-tuple-element.16.q_ref, bf16[1024,128]{1,0:T(8,128)(2,1)S(1)} %get-tuple-element.17.k_ref, bf16[1024,128]{1,0:T(8,128)(2,1)S(1)} %get-tuple-element.18.v_ref, ...), custom_call_target="tpu_custom_call" | custom-call | tf_op jit(solution)/shard_map/pallas_call | solution.py:229
  (1 shorter events, 0.0 us)
Async XLA Ops:
  2.2 17.6 %collective-permute-start = (f32[192,128]{1,0:T(8,128)S(1)}, f32[192,128]{1,0:T(8,128)S(1)}, u32[]{:S(2)}, u32[]{:S(2)}) collective-permute-start(f32[192,128]{1,0:T(8,128)S(1)} %get-tuple-element.22), channel_id=1, source_target_pairs={{0,1},{1,0},{2,3},{3,2},{4,5},{5,4},{6,7},{7,6},{8,9},{9,8},{10,11... | collective-permute-start | bytes 294920 | tf_op jit(solution)/shard_map/ppermute | solution.py:208

commit v7 on v6

--- a/solution.py
+++ b/solution.py
@@ -7,8 +7,7 @@
 from jax.experimental.pallas import tpu as pltpu
 from jax.sharding import PartitionSpec as P
 
-BLOCK = 512
-SUB = 256
+CHUNK = 256
 AXES = ("seq", "inner")
 F32 = jnp.float32
 BF16 = jnp.bfloat16
@@ -45,19 +44,21 @@
     scale_ref[...] = scaling_of(start, half_rows, width)
     for copy in copies:
         copy.wait()
-    kv, back = [], []
-    for b in range(half_rows // BLOCK):
-        rows = pl.ds(b * BLOCK, BLOCK)
+    kv_total, back_total = 0.0, 0.0
+    for c in range(half_rows // CHUNK):
+        rows = pl.ds(c * CHUNK, CHUNK)
         grad = (scale_ref[rows, :] * o_ref[rows, :].astype(F32)).astype(BF16)
         grad_ref[rows, :] = grad
-        kv.append(dot(k_ref[rows, :], v_ref[rows, :], 0, 0))
-        back.append(dot(q_ref[rows, :], grad, 0, 0))
-    keep_ref[:width, :] = kv[0]
-    keep_ref[width:, :] = back[1]
+        kv = dot(k_ref[rows, :], v_ref[rows, :], 0, 0)
+        back = dot(q_ref[rows, :], grad, 0, 0)
+        keep_ref[0, c] = kv
+        keep_ref[1, c] = back
+        kv_total = kv_total + kv
+        back_total = back_total + back
     half = width // 2
     side = lax.axis_index("inner") % 2
-    total_ref[0] = kv[0] + kv[1]
-    total_ref[1] = back[0] + back[1]
+    total_ref[0] = kv_total
+    total_ref[1] = back_total
     own_ref[0] = total_ref[0, pl.ds(side * half, half), :]
     own_ref[1] = total_ref[1, pl.ds(side * half, half), :]
     send_ref[:width, :] = total_ref[side]
@@ -99,35 +100,18 @@
 
 
 def local_kernel(q_ref, k_ref, v_ref, g_ref, att_ref, qg_ref, kg_ref, vg_ref):
-    row = lax.broadcasted_iota(jnp.int32, (SUB, SUB), 0)
-    col = lax.broadcasted_iota(jnp.int32, (SUB, SUB), 1)
+    row = lax.broadcasted_iota(jnp.int32, (CHUNK, CHUNK), 0)
+    col = lax.broadcasted_iota(jnp.int32, (CHUNK, CHUNK), 1)
     causal = row >= col
-    n = BLOCK // SUB
-
-    def masked(scores):
-        left = scores.shape[1] - SUB
-        last = jnp.where(causal, scores[:, left:], 0.0)
-        if left:
-            last = jnp.concatenate([scores[:, :left], last], 1)
-        return last.astype(BF16)
-
-    for b in range(q_ref.shape[0] // BLOCK):
-        weights, scores = [], []
-        for i in range(n):
-            own = pl.ds(b * BLOCK + i * SUB, SUB)
-            before = pl.ds(b * BLOCK, (i + 1) * SUB)
-            weights.append(masked(dot(q_ref[own, :], k_ref[before, :], 1, 1)))
-            scores.append(masked(dot(g_ref[own, :], v_ref[before, :], 1, 1)))
-            att_ref[own, :] = dot(weights[i], v_ref[before, :], 1, 0)
-            qg_ref[own, :] = dot(scores[i], k_ref[before, :], 1, 0)
-        for j in range(n):
-            own = pl.ds(b * BLOCK + j * SUB, SUB)
-            after = pl.ds(b * BLOCK + j * SUB, (n - j) * SUB)
-            cut = slice(j * SUB, (j + 1) * SUB)
-            w = jnp.concatenate([weights[i][:, cut] for i in range(j, n)], 0)
-            s = jnp.concatenate([scores[i][:, cut] for i in range(j, n)], 0)
-            vg_ref[own, :] = dot(w, g_ref[after, :], 0, 0)
-            kg_ref[own, :] = dot(s, q_ref[after, :], 0, 0)
+    for c in range(q_ref.shape[0] // CHUNK):
+        rows = pl.ds(c * CHUNK, CHUNK)
+        q, k, v, g = q_ref[rows, :], k_ref[rows, :], v_ref[rows, :], g_ref[rows, :]
+        w = jnp.where(causal, dot(q, k, 1, 1), 0.0).astype(BF16)
+        s = jnp.where(causal, dot(g, v, 1, 1), 0.0).astype(BF16)
+        att_ref[rows, :] = dot(w, v, 1, 0)
+        qg_ref[rows, :] = dot(s, k, 1, 0)
+        vg_ref[rows, :] = dot(w, g, 0, 0)
+        kg_ref[rows, :] = dot(s, q, 0, 0)
 
 
 def final_kernel(
@@ -144,26 +128,42 @@
     other = got_ref[:width, :]
     kv0 = kv0 + jnp.where(is_second, other, 0.0)
     back1 = back1 + jnp.where(is_second, 0.0, other)
-    kv_used = [kv0.astype(BF16), (kv0 + keep_ref[:width, :]).astype(BF16)]
-    back_used = [(back1 + keep_ref[width:, :]).astype(BF16), back1.astype(BF16)]
+    chunks = half_rows // CHUNK
+    kv_used, back_used = [kv0], [back1]
+    for c in range(chunks - 1):
+        kv_used.append(kv_used[-1] + keep_ref[0, c])
+        back_used.insert(0, back_used[0] + keep_ref[1, chunks - 1 - c])
+    kv_used = [state.astype(BF16) for state in kv_used]
+    back_used = [state.astype(BF16) for state in back_used]
     copies = []
 
-    def put(i, value, rows):
-        buffers[i][rows, :] = value.astype(BF16)
+    def put(i, values, rows):
+        for c, value in values:
+            buffers[i][pl.ds(c * CHUNK, CHUNK), :] = value.astype(BF16)
         copy = pltpu.make_async_copy(
             buffers[i].at[rows, :], outs[i].at[rows, :], sems.at[len(copies)]
         )
         copy.start()
         copies.append(copy)
 
-    for b in range(half_rows // BLOCK):
-        rows = pl.ds(b * BLOCK, BLOCK)
-        q, k, v, g = q_ref[rows, :], k_ref[rows, :], v_ref[rows, :], g_ref[rows, :]
-        att, qg, kg, vg = (ref[rows, :] for ref in local)
-        put(1, qg + dot(g, kv_used[b], 1, 1), rows)
-        put(2, kg + dot(v, back_used[b], 1, 1), rows)
-        put(3, vg + dot(k, back_used[b], 1, 0), rows)
-        put(0, (att + dot(q, kv_used[b], 1, 0)) * scale_ref[rows, :], rows)
+    def at(ref, c):
+        return ref[pl.ds(c * CHUNK, CHUNK), :]
+
+    att, qg, kg, vg = local
+    for b in range(2):
+        part = range(b * chunks // 2, (b + 1) * chunks // 2)
+        rows = pl.ds(b * half_rows // 2, half_rows // 2)
+        put(1, [(c, at(qg, c) + dot(at(g_ref, c), kv_used[c], 1, 1)) for c in part], rows)
+        put(2, [(c, at(kg, c) + dot(at(v_ref, c), back_used[c], 1, 1)) for c in part], rows)
+        put(3, [(c, at(vg, c) + dot(at(k_ref, c), back_used[c], 1, 0)) for c in part], rows)
+        put(
+            0,
+            [
+                (c, (at(att, c) + dot(at(q_ref, c), kv_used[c], 1, 0)) * at(scale_ref, c))
+                for c in part
+            ],
+            rows,
+        )
     for copy in copies:
         copy.wait()
 
@@ -183,10 +183,9 @@
 
 def per_device(pairs, groups, queries, key_vectors, value_vectors, out_grad):
     half_rows, width = queries.shape
-    blocks = half_rows // BLOCK
     rows16 = jax.ShapeDtypeStruct((half_rows, width), BF16)
     rows32 = jax.ShapeDtypeStruct((half_rows, width), F32)
-    states = jax.ShapeDtypeStruct((2 * width, width), F32)
+    states = jax.ShapeDtypeStruct((2, half_rows // CHUNK, width, width), F32)
     half = width // 2
     halves = jax.ShapeDtypeStruct((2, half, width), F32)
     sent = jax.ShapeDtypeStruct((width + half, width), F32)
@@ -211,7 +210,7 @@
         (rows32,) * 4,
         2**24,
         cost_estimate=pl.CostEstimate(
-            flops=12 * half_rows * BLOCK * width, bytes_accessed=2**22, transcendentals=0
+            flops=12 * half_rows * CHUNK * width, bytes_accessed=2**22, transcendentals=0
         ),
     )(q, k, v, grad)
     count = lax.axis_size("seq")
@@ -232,7 +231,7 @@
         2**24,
         out_specs=(in_hbm,) * 4,
         scratch_shapes=[pltpu.VMEM((half_rows, width), BF16)] * 4
-        + [pltpu.SemaphoreType.DMA((4 * blocks,))],
+        + [pltpu.SemaphoreType.DMA((8,))],
     )(q, k, v, grad, scale, state, got, keep, *local)
 
 

time: 43.5 us -> 43.5 us (level)
  no operation moved by 1% of the time
where the time goes in v7:
time: 43.5 us; the launch traced here: 43.3 us
  blocking collectives  22 us (51%)
  starting transfers between devices  16.1 us (37%)
  Pallas kernels  4.51 us (10%)
  between operations  0.68 us (2%)
    ppermute x1, starting transfers between devices, per_device(): got = lax.ppermute(send, AXES, pairs)  16.1 us
    all_to_all x1, blocking collectives, per_device(): parts = lax.all_to_all(parts, 'seq', 0, 0)  14.2 us
    all_to_all x1, blocking collectives, per_device(): state = lax.all_to_all(state, AXES, 0, 0, axis_index_groups=groups)  7.8 us
    pallas_call x1, Pallas kernels, per_device(): call(outer_kernel, (sent, halves, states) + (rows16,) * 4 + (rows32,), 2...  1.61 us
    pallas_call x1, Pallas kernels, per_device(): call(local_kernel, (rows32,) * 4, 2 ** 24, cost_estimate=pl.CostEstimate(...  1.57 us
    pallas_call x1, Pallas kernels, per_device(): call(final_kernel, (rows16,) * 4, 2 ** 24, out_specs=(in_hbm,) * 4, scrat...  1.23 us
  transfers between devices with their start and end apart: 1, of which 0 were waited for; matrix products, arithmetic and copies ran while one was open for 0% of the time, Pallas kernels for 4%

profile of v7, /device:TPU:1, one launch (start us, length us, event | category | flops | bytes accessed | tf_op | source)
XLA Modules:
  0.0 43.3 jit_solution(8148022616548609887)
XLA Ops:
  0.6 1.6 %shard_map.75 = (f32[192,128]{1,0:T(8,128)S(1)}, f32[2,64,128]{2,1,0:T(8,128)S(1)}, f32[2,4,128,128]{3,2,1,0:T(8,128)S(1)}, bf16[1024,128]{1,0:T(8,128)(2,1)S(1)...) custom-call(bf16[1024,128]{1,0:T(8,128)(2,1)} %q_hbm.1, ...), custom_call_target="tpu_custom_call" | custom-call | tf_op jit(solution)/shard_map/pallas_call | solution.py:195
  2.2 16.1 %collective-permute-start = (f32[192,128]{1,0:T(8,128)S(1)}, f32[192,128]{1,0:T(8,128)S(1)}, u32[]{:S(2)}, u32[]{:S(2)}) collective-permute-start(f32[192,128]{1,0:T(8,128)S(1)} %get-tuple-element.22), channel_id=1, source_target_pairs={{0,1},{1,0},{2,3},{3,2},{4,5},{5,4},{6,7},{7,6},{8,9},{9,8},{10,11... | collective-permute-start | bytes 294920 | tf_op jit(solution)/shard_map/ppermute | solution.py:207
  18.3 1.6 %shard_map.76 = (f32[1024,128]{1,0:T(8,128)S(1)}, f32[1024,128]{1,0:T(8,128)S(1)}, f32[1024,128]{1,0:T(8,128)S(1)}, f32[1024,128]{1,0:T(8,128)S(1)}) custom-call(bf16[1024,128]{1,0:T(8,128)(2,1)S(1)} %get-tuple-element.16.q_ref, bf16[1024,128]{1,0:T(8,128)(2,1)S(1)} %get-tuple-element.17.k_ref, bf16[1024,128]{1,0:T(8,128)(2,1)S(1)} %get-tuple-element.18.v_ref, ...), custom_call_target="tpu_custom_call" | custom-call | flops 402653184 | bytes 4194304 | tf_op jit(solution)/shard_map/pallas_call | solution.py:208
  19.9 0.0 collective-permute-done.got_ref
  20.0 14.2 %all_to_all.10.parts_ref = f32[16,32,128]{2,1,0:T(8,128)S(1)} all-to-all(f32[16,32,128]{2,1,0:T(8,128)S(1)} %shard_map.77), channel_id=1, replica_groups=mesh['seq'=16,'inner'=64] {'seq'}, dimensions={0} | all-to-all | bytes 524288 | tf_op jit(solution)/shard_map/all_to_all | solution.py:224
  34.2 0.1 shard_map.78
  34.2 7.8 %all_to_all.11.state_ref = f32[4,2,32,128]{3,2,1,0:T(8,128)S(1)} all-to-all(f32[4,2,32,128]{3,2,1,0:T(8,128)S(1)} %shard_map.78), channel_id=1, replica_groups={{0,1,64,65},{2,3,66,67},{4,5,68,69},{6,7,70,71},{8,9,72,73},{10,11,74,7..., dimensions={0} | all-to-all | bytes 262144 | tf_op jit(solution)/shard_map/all_to_all | solution.py:227
  42.0 1.2 %shard_map.79 = (bf16[1024,128]{1,0:T(8,128)(2,1)}, bf16[1024,128]{1,0:T(8,128)(2,1)}, bf16[1024,128]{1,0:T(8,128)(2,1)}, bf16[1024,128]{1,0:T(8,128)(2,1)}) custom-call(bf16[1024,128]{1,0:T(8,128)(2,1)S(1)} %get-tuple-element.16.q_ref, bf16[1024,128]{1,0:T(8,128)(2,1)S(1)} %get-tuple-element.17.k_ref, bf16[1024,128]{1,0:T(8,128)(2,1)S(1)} %get-tuple-element.18.v_ref, ...), custom_call_target="tpu_custom_call" | custom-call | tf_op jit(solution)/shard_map/pallas_call | solution.py:228
  (1 shorter events, 0.0 us)
Async XLA Ops:
  2.2 17.6 %collective-permute-start = (f32[192,128]{1,0:T(8,128)S(1)}, f32[192,128]{1,0:T(8,128)S(1)}, u32[]{:S(2)}, u32[]{:S(2)}) collective-permute-start(f32[192,128]{1,0:T(8,128)S(1)} %get-tuple-element.22), channel_id=1, source_target_pairs={{0,1},{1,0},{2,3},{3,2},{4,5},{5,4},{6,7},{7,6},{8,9},{9,8},{10,11... | collective-permute-start | bytes 294920 | tf_op jit(solution)/shard_map/ppermute | solution.py:207

commit v8 on v6

--- a/solution.py
+++ b/solution.py
@@ -80,7 +80,7 @@
         out_ref[i] = jnp.where(takes_kv, kv[cut], back[cut])
 
 
-def gather_kernel(parts_ref, send_ref):
+def gather_kernel(parts_ref, send_ref, mine_ref):
     pair = lax.axis_index("seq") // 2
     zero = jnp.zeros(parts_ref.shape[1:], F32)
     earlier, later = zero, zero
@@ -89,16 +89,24 @@
         earlier = earlier + jnp.where(i // 2 < pair, parts_ref[i], zero)
         j = count - 1 - i
         later = later + jnp.where(j // 2 > pair, parts_ref[j], zero)
+    is_first = lax.axis_index("seq") % 2 == 0
     with_first = earlier + parts_ref[2 * pair]
     with_second = later + parts_ref[2 * pair + 1]
-    for side in range(2):
-        send_ref[side, 0] = earlier
-        send_ref[side, 1] = with_second
-        send_ref[2 + side, 0] = with_first
-        send_ref[2 + side, 1] = later
-
-
-def local_kernel(q_ref, k_ref, v_ref, g_ref, att_ref, qg_ref, kg_ref, vg_ref):
+    mine_ref[0] = jnp.where(is_first, earlier, with_first)
+    mine_ref[1] = jnp.where(is_first, with_second, later)
+    send_ref[0] = jnp.where(is_first, with_first, earlier)
+    send_ref[1] = jnp.where(is_first, later, with_second)
+
+
+def join_kernel(mine_ref, got_ref, out_ref):
+    rows = mine_ref.shape[1]
+    place = lax.axis_index("seq") % 2
+    for i in range(2):
+        out_ref[i, pl.ds(place * rows, rows), :] = mine_ref[i]
+        out_ref[i, pl.ds((1 - place) * rows, rows), :] = got_ref[i]
+
+
+def local_kernel(q_ref, k_ref, v_ref, g_ref, after_ref, att_ref, qg_ref, kg_ref, vg_ref):
     row = lax.broadcasted_iota(jnp.int32, (SUB, SUB), 0)
     col = lax.broadcasted_iota(jnp.int32, (SUB, SUB), 1)
     causal = row >= col
@@ -131,14 +139,20 @@
 
 
 def final_kernel(
-    q_ref, k_ref, v_ref, g_ref, scale_ref, state_ref, got_ref, keep_ref, *refs
+    q_ref, k_ref, v_ref, g_ref, scale_ref, mine_ref, theirs_ref, got_ref, keep_ref, *refs
 ):
     local, outs = refs[:4], refs[4:8]
     buffers, sems = refs[8:12], refs[12]
     half_rows, width = q_ref.shape
     is_second = lax.axis_index("inner") % 2 == 1
     kv0, back1 = (
-        jnp.concatenate([state_ref[2 * z + c, i] for c in range(2) for z in range(2)], 0)
+        jnp.concatenate(
+            [
+                jnp.where(is_second, theirs_ref[i], mine_ref[i]),
+                jnp.where(is_second, mine_ref[i], theirs_ref[i]),
+            ],
+            0,
+        )
         for i in range(2)
     )
     other = got_ref[:width, :]
@@ -181,7 +195,7 @@
     )
 
 
-def per_device(pairs, groups, queries, key_vectors, value_vectors, out_grad):
+def per_device(sides, neighbours, queries, key_vectors, value_vectors, out_grad):
     half_rows, width = queries.shape
     blocks = half_rows // BLOCK
     rows16 = jax.ShapeDtypeStruct((half_rows, width), BF16)
@@ -205,27 +219,27 @@
         ],
     )(*(in_memory(x) for x in (queries, key_vectors, value_vectors, out_grad)))
 
-    got = lax.ppermute(send, AXES, pairs)
+    got = lax.ppermute(send, AXES, sides)
+    count = lax.axis_size("seq")
+    quarter = half // 2
+    parts = call(
+        spread_kernel, jax.ShapeDtypeStruct((count, quarter, width), F32), 2**23
+    )(own, got)
+    parts = lax.all_to_all(parts, "seq", 0, 0)
+    quarters = jax.ShapeDtypeStruct((2, quarter, width), F32)
+    send, mine = call(gather_kernel, (quarters,) * 2, 2**23)(parts)
+    near = lax.ppermute(send, AXES, neighbours)
     local = call(
         local_kernel,
         (rows32,) * 4,
         2**24,
+        in_specs=[in_vmem] * 4 + [anywhere],
         cost_estimate=pl.CostEstimate(
             flops=12 * half_rows * BLOCK * width, bytes_accessed=2**22, transcendentals=0
         ),
-    )(q, k, v, grad)
-    count = lax.axis_size("seq")
-    quarter = half // 2
-    parts = call(
-        spread_kernel,
-        jax.ShapeDtypeStruct((count, quarter, width), F32),
-        2**23,
-        in_specs=[in_vmem] * 2 + [anywhere],
-    )(own, got, local[0])
-    parts = lax.all_to_all(parts, "seq", 0, 0)
-    quads = jax.ShapeDtypeStruct((4, 2, quarter, width), F32)
-    state = call(gather_kernel, quads, 2**23)(parts)
-    state = lax.all_to_all(state, AXES, 0, 0, axis_index_groups=groups)
+    )(q, k, v, grad, mine)
+    mine = call(join_kernel, halves, 2**23)(mine, near)
+    theirs = lax.ppermute(mine, AXES, sides)
     return call(
         final_kernel,
         (rows16,) * 4,
@@ -233,20 +247,18 @@
         out_specs=(in_hbm,) * 4,
         scratch_shapes=[pltpu.VMEM((half_rows, width), BF16)] * 4
         + [pltpu.SemaphoreType.DMA((4 * blocks,))],
-    )(q, k, v, grad, scale, state, got, keep, *local)
+    )(q, k, v, grad, scale, mine, theirs, got, keep, *local)
 
 
 def solution(mesh):
     n_seq, n_inner = mesh.shape["seq"], mesh.shape["inner"]
-    pairs = [(i, i ^ 1) for i in range(n_seq * n_inner)]
-    groups = [
-        [(2 * x + z) * n_inner + 2 * h + side for z in range(2) for side in range(2)]
-        for x in range(n_seq // 2)
-        for h in range(n_inner // 2)
+    sides = [(i, i ^ 1) for i in range(n_seq * n_inner)]
+    neighbours = [
+        (s * n_inner + i, (s ^ 1) * n_inner + i) for s in range(n_seq) for i in range(n_inner)
     ]
     spec = P("seq", "inner")
     return jax.shard_map(
-        functools.partial(per_device, pairs, groups),
+        functools.partial(per_device, sides, neighbours),
         mesh=mesh,
         in_specs=(spec,) * 4,
         out_specs=(spec,) * 4,

time: 43.5 us -> 46.2 us (1.062)
  blocking collectives: 22 us -> 13.9 us
  starting transfers between devices: 16.1 us -> 23.2 us
  waiting for transfers between devices: 0.01 us -> 3.58 us
    all_to_all x1 -> x0, blocking collectives: 7.8 us -> none  [per_device(): state = lax.all_to_all(state, AXES, 0, 0, axis_index_groups=groups)]
    ppermute x1 -> x3, starting transfers between devices: 16.1 us -> 23.2 us  [the longest x1 16.1 us: per_device(): got = lax.ppermute(send, AXES, sides)]
    ppermute x1 -> x3, waiting for transfers between devices: 0.01 us -> 3.58 us  [the longest x1 2.66 us: per_device(): near = lax.ppermute(send, AXES, neighbours)]
    pallas_call x2 -> x3, Pallas kernels: 1.59 us -> 1.61 us  [the longest x1 1.54 us: per_device(): call(local_kernel, (rows32,) * 4, 2 ** 24, in_specs=[in_vmem] * 4 + [anyw...]
  transfers between devices with their start and end apart: 1 -> 3, of which waited for: 0 -> 2; matrix products, arithmetic and copies ran while one was open for 0% -> 0% of each run, Pallas kernels for 4% -> 3%
where the time goes in v8:
time: 46.2 us; the launch traced here: 45.9 us
  starting transfers between devices  23.2 us (50%)
  blocking collectives  13.9 us (30%)
  Pallas kernels  4.51 us (10%)
  waiting for transfers between devices  3.58 us (8%)
  between operations  0.69 us (1%)
    ppermute x1, starting transfers between devices, per_device(): got = lax.ppermute(send, AXES, sides)  16.1 us
    all_to_all x1, blocking collectives, per_device(): parts = lax.all_to_all(parts, 'seq', 0, 0)  13.9 us
    ppermute x1, starting transfers between devices, per_device(): theirs = lax.ppermute(mine, AXES, sides)  5.15 us
    ppermute x1, waiting for transfers between devices, per_device(): near = lax.ppermute(send, AXES, neighbours)  2.66 us
    ppermute x1, starting transfers between devices, per_device(): near = lax.ppermute(send, AXES, neighbours)  2 us
    pallas_call x1, Pallas kernels, per_device(): call(outer_kernel, (sent, halves, states) + (rows16,) * 4 + (rows32,), 2...  1.59 us
    pallas_call x1, Pallas kernels, per_device(): call(local_kernel, (rows32,) * 4, 2 ** 24, in_specs=[in_vmem] * 4 + [anyw...  1.54 us
    pallas_call x1, Pallas kernels, per_device(): call(final_kernel, (rows16,) * 4, 2 ** 24, out_specs=(in_hbm,) * 4, scrat...  1.28 us
  transfers between devices with their start and end apart: 3, of which 2 were waited for; matrix products, arithmetic and copies ran while one was open for 0% of the time, Pallas kernels for 3%

profile of v8, /device:TPU:1, one launch (start us, length us, event | category | flops | bytes accessed | tf_op | source)
XLA Modules:
  0.0 45.9 jit_solution(7298973692803393080)
XLA Ops:
  0.6 1.6 %shard_map.75 = (f32[192,128]{1,0:T(8,128)S(1)}, f32[2,64,128]{2,1,0:T(8,128)S(1)}, f32[256,128]{1,0:T(8,128)S(1)}, bf16[1024,128]{1,0:T(8,128)(2,1)S(1)}, bf16[...) custom-call(bf16[1024,128]{1,0:T(8,128)(2,1)} %q_hbm.1, ...), custom_call_target="tpu_custom_call" | custom-call | tf_op jit(solution)/shard_map/pallas_call | solution.py:210
  2.2 16.1 %collective-permute-start = (f32[192,128]{1,0:T(8,128)S(1)}, f32[192,128]{1,0:T(8,128)S(1)}, u32[]{:S(2)}, u32[]{:S(2)}) collective-permute-start(f32[192,128]{1,0:T(8,128)S(1)} %get-tuple-element.24), channel_id=1, source_target_pairs={{0,1},{1,0},{2,3},{3,2},{4,5},{5,4},{6,7},{7,6},{8,9},{9,8},{10,11... | collective-permute-start | bytes 294920 | tf_op jit(solution)/shard_map/ppermute | solution.py:222
  18.3 0.9 %collective-permute-done.got_ref = f32[192,128]{1,0:T(8,128)S(1)} collective-permute-done((f32[192,128]{1,0:T(8,128)S(1)}, f32[192,128]{1,0:T(8,128)S(1)}, u32[]{:S(2)}, u32[]{:S(2)}) %collective-permute-start) | collective-permute-done | bytes 98336 | tf_op jit(solution)/shard_map/ppermute | solution.py:222
  19.3 13.9 %all_to_all.5.parts_ref = f32[16,32,128]{2,1,0:T(8,128)S(1)} all-to-all(f32[16,32,128]{2,1,0:T(8,128)S(1)} %shard_map.76), channel_id=1, replica_groups=mesh['seq'=16,'inner'=64] {'seq'}, dimensions={0} | all-to-all | bytes 524288 | tf_op jit(solution)/shard_map/all_to_all | solution.py:228
  33.2 0.1 shard_map.77
  33.3 2.0 %collective-permute-start.1 = (f32[2,32,128]{2,1,0:T(8,128)S(1)}, f32[2,32,128]{2,1,0:T(8,128)S(1)}, u32[]{:S(2)}, u32[]{:S(2)}) collective-permute-start(f32[2,32,128]{2,1,0:T(8,128)S(1)} %get-tuple-element.26), channel_id=1, source_target_pairs={{0,64},{1,65},{2,66},{3,67},{4,68},{5,69},{6,70},{7,71},{8,72},{9,... | collective-permute-start | bytes 98312 | tf_op jit(solution)/shard_map/ppermute | solution.py:231
  35.3 2.7 %collective-permute-done.1.got_ref = f32[2,32,128]{2,1,0:T(8,128)S(1)} collective-permute-done((f32[2,32,128]{2,1,0:T(8,128)S(1)}, f32[2,32,128]{2,1,0:T(8,128)S(1)}, u32[]{:S(2)}, u32[]{:S(2)}) %collective-permute-start.1) | collective-permute-done | bytes 32800 | tf_op jit(solution)/shard_map/ppermute | solution.py:231
  37.9 5.1 %collective-permute-start.2 = (f32[2,64,128]{2,1,0:T(8,128)S(1)}, f32[2,64,128]{2,1,0:T(8,128)S(1)}, u32[]{:S(2)}, u32[]{:S(2)}) collective-permute-start(f32[2,64,128]{2,1,0:T(8,128)S(1)} %shard_map.78.mine_ref), channel_id=1, source_target_pairs={{0,1},{1,0},{2,3},{3,2},{4,5},{5,4},{6,7},{7,6},{8,9},{9,8},{10,11... | collective-permute-start | bytes 196616 | tf_op jit(solution)/shard_map/ppermute | solution.py:242
  43.1 1.5 %shard_map.79 = (f32[1024,128]{1,0:T(8,128)S(1)}, f32[1024,128]{1,0:T(8,128)S(1)}, f32[1024,128]{1,0:T(8,128)S(1)}, f32[1024,128]{1,0:T(8,128)S(1)}) custom-call(bf16[1024,128]{1,0:T(8,128)(2,1)S(1)} %get-tuple-element.18.q_ref, bf16[1024,128]{1,0:T(8,128)(2,1)S(1)} %get-tuple-element.19.k_ref, bf16[1024,128]{1,0:T(8,128)(2,1)S(1)} %get-tuple-element.20.v_ref, ...), custom_call_target="tpu_custom_call" | custom-call | flops 805306368 | bytes 4194304 | tf_op jit(solution)/shard_map/pallas_call | solution.py:232
  44.6 0.0 collective-permute-done.2.theirs_ref
  44.6 1.3 %shard_map.80 = (bf16[1024,128]{1,0:T(8,128)(2,1)}, bf16[1024,128]{1,0:T(8,128)(2,1)}, bf16[1024,128]{1,0:T(8,128)(2,1)}, bf16[1024,128]{1,0:T(8,128)(2,1)}) custom-call(bf16[1024,128]{1,0:T(8,128)(2,1)S(1)} %get-tuple-element.18.q_ref, bf16[1024,128]{1,0:T(8,128)(2,1)S(1)} %get-tuple-element.19.k_ref, bf16[1024,128]{1,0:T(8,128)(2,1)S(1)} %get-tuple-element.20.v_ref, ...), custom_call_target="tpu_custom_call" | custom-call | tf_op jit(solution)/shard_map/pallas_call | solution.py:243
  (2 shorter events, 0.0 us)
Async XLA Ops:
  2.2 17.0 %collective-permute-start = (f32[192,128]{1,0:T(8,128)S(1)}, f32[192,128]{1,0:T(8,128)S(1)}, u32[]{:S(2)}, u32[]{:S(2)}) collective-permute-start(f32[192,128]{1,0:T(8,128)S(1)} %get-tuple-element.24), channel_id=1, source_target_pairs={{0,1},{1,0},{2,3},{3,2},{4,5},{5,4},{6,7},{7,6},{8,9},{9,8},{10,11... | collective-permute-start | bytes 294920 | tf_op jit(solution)/shard_map/ppermute | solution.py:222
  33.3 4.7 %collective-permute-start.1 = (f32[2,32,128]{2,1,0:T(8,128)S(1)}, f32[2,32,128]{2,1,0:T(8,128)S(1)}, u32[]{:S(2)}, u32[]{:S(2)}) collective-permute-start(f32[2,32,128]{2,1,0:T(8,128)S(1)} %get-tuple-element.26), channel_id=1, source_target_pairs={{0,64},{1,65},{2,66},{3,67},{4,68},{5,69},{6,70},{7,71},{8,72},{9,... | collective-permute-start | bytes 98312 | tf_op jit(solution)/shard_map/ppermute | solution.py:231
  37.9 6.7 %collective-permute-start.2 = (f32[2,64,128]{2,1,0:T(8,128)S(1)}, f32[2,64,128]{2,1,0:T(8,128)S(1)}, u32[]{:S(2)}, u32[]{:S(2)}) collective-permute-start(f32[2,64,128]{2,1,0:T(8,128)S(1)} %shard_map.78.mine_ref), channel_id=1, source_target_pairs={{0,1},{1,0},{2,3},{3,2},{4,5},{5,4},{6,7},{7,6},{8,9},{9,8},{10,11... | collective-permute-start | bytes 196616 | tf_op jit(solution)/shard_map/ppermute | solution.py:242

commit v9 on v6

--- a/solution.py
+++ b/solution.py
@@ -28,9 +28,55 @@
     return (lax.axis_index("seq") * 2 + lax.axis_index("inner") % 2) * half_rows
 
 
+def waits_at_start():
+    place = lax.axis_index("inner")
+    near = (place > 0) & (place < lax.axis_size("inner") // 4)
+    return (lax.axis_index("seq") == 0) & near
+
+
+def in_block(q_ref, k_ref, v_ref, g_ref, outs):
+    att_ref, qg_ref, kg_ref, vg_ref = outs
+    row = lax.broadcasted_iota(jnp.int32, (SUB, SUB), 0)
+    col = lax.broadcasted_iota(jnp.int32, (SUB, SUB), 1)
+    causal = row >= col
+    n = BLOCK // SUB
+    blocks = range(q_ref.shape[0] // BLOCK)
+
+    def tiles(b, first, count):
+        return pl.ds(b * BLOCK + first * SUB, count * SUB)
+
+    def masked(scores):
+        left = scores.shape[1] - SUB
+        last = jnp.where(causal, scores[:, left:], 0.0)
+        if left:
+            last = jnp.concatenate([scores[:, :left], last], 1)
+        return last.astype(BF16)
+
+    weights, scores = {}, {}
+    for b in blocks:
+        for i in range(n):
+            own, before = tiles(b, i, 1), tiles(b, 0, i + 1)
+            weights[b, i] = masked(dot(q_ref[own, :], k_ref[before, :], 1, 1))
+            scores[b, i] = masked(dot(g_ref[own, :], v_ref[before, :], 1, 1))
+    for b in blocks:
+        for i in range(n):
+            own, before = tiles(b, i, 1), tiles(b, 0, i + 1)
+            att_ref[own, :] = dot(weights[b, i], v_ref[before, :], 1, 0)
+            qg_ref[own, :] = dot(scores[b, i], k_ref[before, :], 1, 0)
+    for b in blocks:
+        for j in range(n):
+            own, after = tiles(b, j, 1), tiles(b, j, n - j)
+            cut = slice(j * SUB, (j + 1) * SUB)
+            w = jnp.concatenate([weights[b, i][:, cut] for i in range(j, n)], 0)
+            s = jnp.concatenate([scores[b, i][:, cut] for i in range(j, n)], 0)
+            vg_ref[own, :] = dot(w, g_ref[after, :], 0, 0)
+            kg_ref[own, :] = dot(s, q_ref[after, :], 0, 0)
+
+
 def outer_kernel(
     q_hbm, k_hbm, v_hbm, o_hbm,
     send_ref, own_ref, keep_ref, q_ref, k_ref, v_ref, grad_ref, scale_ref,
+    att_ref, qg_ref, kg_ref, vg_ref,
     o_ref, total_ref, sems,
 ):
     half_rows, width = q_ref.shape
@@ -63,9 +109,12 @@
     send_ref[:width, :] = total_ref[side]
     send_ref[width:, :] = total_ref[1 - side, pl.ds((1 - side) * half, half), :]
 
-
-def spread_kernel(own_ref, got_ref, *refs):
-    out_ref = refs[-1]
+    @pl.when(waits_at_start())
+    def _():
+        in_block(q_ref, k_ref, v_ref, grad_ref, (att_ref, qg_ref, kg_ref, vg_ref))
+
+
+def spread_kernel(own_ref, got_ref, out_ref):
     count, rows, width = out_ref.shape
     half = width // 2
     me = lax.axis_index("seq")
@@ -98,43 +147,11 @@
         send_ref[2 + side, 1] = later
 
 
-def local_kernel(q_ref, k_ref, v_ref, g_ref, att_ref, qg_ref, kg_ref, vg_ref):
-    row = lax.broadcasted_iota(jnp.int32, (SUB, SUB), 0)
-    col = lax.broadcasted_iota(jnp.int32, (SUB, SUB), 1)
-    causal = row >= col
-    n = BLOCK // SUB
-
-    def masked(scores):
-        left = scores.shape[1] - SUB
-        last = jnp.where(causal, scores[:, left:], 0.0)
-        if left:
-            last = jnp.concatenate([scores[:, :left], last], 1)
-        return last.astype(BF16)
-
-    for b in range(q_ref.shape[0] // BLOCK):
-        weights, scores = [], []
-        for i in range(n):
-            own = pl.ds(b * BLOCK + i * SUB, SUB)
-            before = pl.ds(b * BLOCK, (i + 1) * SUB)
-            weights.append(masked(dot(q_ref[own, :], k_ref[before, :], 1, 1)))
-            scores.append(masked(dot(g_ref[own, :], v_ref[before, :], 1, 1)))
-            att_ref[own, :] = dot(weights[i], v_ref[before, :], 1, 0)
-            qg_ref[own, :] = dot(scores[i], k_ref[before, :], 1, 0)
-        for j in range(n):
-            own = pl.ds(b * BLOCK + j * SUB, SUB)
-            after = pl.ds(b * BLOCK + j * SUB, (n - j) * SUB)
-            cut = slice(j * SUB, (j + 1) * SUB)
-            w = jnp.concatenate([weights[i][:, cut] for i in range(j, n)], 0)
-            s = jnp.concatenate([scores[i][:, cut] for i in range(j, n)], 0)
-            vg_ref[own, :] = dot(w, g_ref[after, :], 0, 0)
-            kg_ref[own, :] = dot(s, q_ref[after, :], 0, 0)
-
-
 def final_kernel(
     q_ref, k_ref, v_ref, g_ref, scale_ref, state_ref, got_ref, keep_ref, *refs
 ):
     local, outs = refs[:4], refs[4:8]
-    buffers, sems = refs[8:12], refs[12]
+    buffers, here, sems = refs[8:12], refs[12:16], refs[16]
     half_rows, width = q_ref.shape
     is_second = lax.axis_index("inner") % 2 == 1
     kv0, back1 = (
@@ -146,26 +163,39 @@
     back1 = back1 + jnp.where(is_second, 0.0, other)
     kv_used = [kv0.astype(BF16), (kv0 + keep_ref[:width, :]).astype(BF16)]
     back_used = [(back1 + keep_ref[width:, :]).astype(BF16), back1.astype(BF16)]
-    copies = []
-
-    def put(i, value, rows):
-        buffers[i][rows, :] = value.astype(BF16)
-        copy = pltpu.make_async_copy(
-            buffers[i].at[rows, :], outs[i].at[rows, :], sems.at[len(copies)]
-        )
-        copy.start()
-        copies.append(copy)
-
-    for b in range(half_rows // BLOCK):
-        rows = pl.ds(b * BLOCK, BLOCK)
-        q, k, v, g = q_ref[rows, :], k_ref[rows, :], v_ref[rows, :], g_ref[rows, :]
-        att, qg, kg, vg = (ref[rows, :] for ref in local)
-        put(1, qg + dot(g, kv_used[b], 1, 1), rows)
-        put(2, kg + dot(v, back_used[b], 1, 1), rows)
-        put(3, vg + dot(k, back_used[b], 1, 0), rows)
-        put(0, (att + dot(q, kv_used[b], 1, 0)) * scale_ref[rows, :], rows)
-    for copy in copies:
-        copy.wait()
+
+    def finish(local):
+        copies = []
+
+        def put(i, value, rows):
+            buffers[i][rows, :] = value.astype(BF16)
+            copy = pltpu.make_async_copy(
+                buffers[i].at[rows, :], outs[i].at[rows, :], sems.at[len(copies)]
+            )
+            copy.start()
+            copies.append(copy)
+
+        for b in range(half_rows // BLOCK):
+            rows = pl.ds(b * BLOCK, BLOCK)
+            q, k, v, g = q_ref[rows, :], k_ref[rows, :], v_ref[rows, :], g_ref[rows, :]
+            att, qg, kg, vg = (ref[rows, :] for ref in local)
+            put(1, qg + dot(g, kv_used[b], 1, 1), rows)
+            put(2, kg + dot(v, back_used[b], 1, 1), rows)
+            put(3, vg + dot(k, back_used[b], 1, 0), rows)
+            put(0, (att + dot(q, kv_used[b], 1, 0)) * scale_ref[rows, :], rows)
+        for copy in copies:
+            copy.wait()
+
+    ready = waits_at_start()
+
+    @pl.when(ready)
+    def _():
+        finish(local)
+
+    @pl.when(jnp.logical_not(ready))
+    def _():
+        in_block(q_ref, k_ref, v_ref, g_ref, here)
+        finish(here)
 
 
 def in_memory(array):
@@ -191,12 +221,10 @@
     halves = jax.ShapeDtypeStruct((2, half, width), F32)
     sent = jax.ShapeDtypeStruct((width + half, width), F32)
     in_hbm = pl.BlockSpec(memory_space=pltpu.HBM)
-    in_vmem = pl.BlockSpec(memory_space=pltpu.VMEM)
-    anywhere = pl.BlockSpec(memory_space=pl.ANY)
-    send, own, keep, q, k, v, grad, scale = call(
+    send, own, keep, q, k, v, grad, scale, *local = call(
         outer_kernel,
-        (sent, halves, states) + (rows16,) * 4 + (rows32,),
-        2**23,
+        (sent, halves, states) + (rows16,) * 4 + (rows32,) * 5,
+        2**24,
         in_specs=[in_hbm] * 4,
         scratch_shapes=[
             pltpu.VMEM((half_rows, width), BF16),
@@ -206,22 +234,13 @@
     )(*(in_memory(x) for x in (queries, key_vectors, value_vectors, out_grad)))
 
     got = lax.ppermute(send, AXES, pairs)
-    local = call(
-        local_kernel,
-        (rows32,) * 4,
-        2**24,
-        cost_estimate=pl.CostEstimate(
-            flops=12 * half_rows * BLOCK * width, bytes_accessed=2**22, transcendentals=0
-        ),
-    )(q, k, v, grad)
     count = lax.axis_size("seq")
     quarter = half // 2
     parts = call(
         spread_kernel,
         jax.ShapeDtypeStruct((count, quarter, width), F32),
         2**23,
-        in_specs=[in_vmem] * 2 + [anywhere],
-    )(own, got, local[0])
+    )(own, got)
     parts = lax.all_to_all(parts, "seq", 0, 0)
     quads = jax.ShapeDtypeStruct((4, 2, quarter, width), F32)
     state = call(gather_kernel, quads, 2**23)(parts)
@@ -232,6 +251,7 @@
         2**24,
         out_specs=(in_hbm,) * 4,
         scratch_shapes=[pltpu.VMEM((half_rows, width), BF16)] * 4
+        + [pltpu.VMEM((half_rows, width), F32)] * 4
         + [pltpu.SemaphoreType.DMA((4 * blocks,))],
     )(q, k, v, grad, scale, state, got, keep, *local)
 

time: 43.5 us -> 42.8 us (0.984)
  starting transfers between devices: 16.1 us -> 14.7 us
  waiting for transfers between devices: 0.01 us -> 0.92 us
    ppermute x1, starting transfers between devices: 16.1 us -> 14.7 us  [per_device(): got = lax.ppermute(send, AXES, pairs)]
    ppermute x1, waiting for transfers between devices: 0.01 us -> 0.92 us  [per_device(): got = lax.ppermute(send, AXES, pairs)]
    pallas_call x2 -> x1, Pallas kernels: 3.13 us -> 2.99 us  [per_device(): call(outer_kernel, (sent, halves, states) + (rows16,) * 4 + (rows32,) * 5...]
  transfers between devices with their start and end apart: 1 -> 1, of which waited for: 0 -> 1; matrix products, arithmetic and copies ran while one was open for 0% -> 0% of each run, Pallas kernels for 4% -> 0%
where the time goes in v9:
time: 42.8 us; the launch traced here: 42.6 us
  blocking collectives  22 us (51%)
  starting transfers between devices  14.7 us (34%)
  Pallas kernels  4.36 us (10%)
  waiting for transfers between devices  0.92 us (2%)
  between operations  0.66 us (2%)
    ppermute x1, starting transfers between devices, per_device(): got = lax.ppermute(send, AXES, pairs)  14.7 us
    all_to_all x1, blocking collectives, per_device(): parts = lax.all_to_all(parts, 'seq', 0, 0)  13.9 us
    all_to_all x1, blocking collectives, per_device(): state = lax.all_to_all(state, AXES, 0, 0, axis_index_groups=groups)  8.07 us
    pallas_call x1, Pallas kernels, per_device(): call(outer_kernel, (sent, halves, states) + (rows16,) * 4 + (rows32,) * 5...  2.99 us
    pallas_call x1, Pallas kernels, per_device(): call(final_kernel, (rows16,) * 4, 2 ** 24, out_specs=(in_hbm,) * 4, scrat...  1.28 us
    ppermute x1, waiting for transfers between devices, per_device(): got = lax.ppermute(send, AXES, pairs)  0.92 us
  transfers between devices with their start and end apart: 1, of which 1 were waited for; matrix products, arithmetic and copies ran while one was open for 0% of the time, Pallas kernels for 0%

profile of v9, /device:TPU:1, one launch (start us, length us, event | category | flops | bytes accessed | tf_op | source)
XLA Modules:
  0.0 42.6 jit_solution(8314653127727088908)
XLA Ops:
  0.6 3.0 %shard_map.75 = (f32[192,128]{1,0:T(8,128)S(1)}, f32[2,64,128]{2,1,0:T(8,128)S(1)}, f32[256,128]{1,0:T(8,128)S(1)}, bf16[1024,128]{1,0:T(8,128)(2,1)S(1)}, bf16[...) custom-call(bf16[1024,128]{1,0:T(8,128)(2,1)} %q_hbm.1, ...), custom_call_target="tpu_custom_call" | custom-call | tf_op jit(solution)/shard_map/pallas_call | solution.py:224
  3.6 14.7 %collective-permute-start = (f32[192,128]{1,0:T(8,128)S(1)}, f32[192,128]{1,0:T(8,128)S(1)}, u32[]{:S(2)}, u32[]{:S(2)}) collective-permute-start(f32[192,128]{1,0:T(8,128)S(1)} %get-tuple-element.22), channel_id=1, source_target_pairs={{0,1},{1,0},{2,3},{3,2},{4,5},{5,4},{6,7},{7,6},{8,9},{9,8},{10,11... | collective-permute-start | bytes 294920 | tf_op jit(solution)/shard_map/ppermute | solution.py:236
  18.3 0.9 %collective-permute-done.got_ref = f32[192,128]{1,0:T(8,128)S(1)} collective-permute-done((f32[192,128]{1,0:T(8,128)S(1)}, f32[192,128]{1,0:T(8,128)S(1)}, u32[]{:S(2)}, u32[]{:S(2)}) %collective-permute-start) | collective-permute-done | bytes 98336 | tf_op jit(solution)/shard_map/ppermute | solution.py:236
  19.3 13.9 %all_to_all.10.parts_ref = f32[16,32,128]{2,1,0:T(8,128)S(1)} all-to-all(f32[16,32,128]{2,1,0:T(8,128)S(1)} %shard_map.76), channel_id=1, replica_groups=mesh['seq'=16,'inner'=64] {'seq'}, dimensions={0} | all-to-all | bytes 524288 | tf_op jit(solution)/shard_map/all_to_all | solution.py:244
  33.2 0.1 shard_map.77
  33.3 8.1 %all_to_all.11.state_ref = f32[4,2,32,128]{3,2,1,0:T(8,128)S(1)} all-to-all(f32[4,2,32,128]{3,2,1,0:T(8,128)S(1)} %shard_map.77), channel_id=1, replica_groups={{0,1,64,65},{2,3,66,67},{4,5,68,69},{6,7,70,71},{8,9,72,73},{10,11,74,7..., dimensions={0} | all-to-all | bytes 262144 | tf_op jit(solution)/shard_map/all_to_all | solution.py:247
  41.3 1.3 %shard_map.78 = (bf16[1024,128]{1,0:T(8,128)(2,1)}, bf16[1024,128]{1,0:T(8,128)(2,1)}, bf16[1024,128]{1,0:T(8,128)(2,1)}, bf16[1024,128]{1,0:T(8,128)(2,1)}) custom-call(bf16[1024,128]{1,0:T(8,128)(2,1)S(1)} %get-tuple-element.16.q_ref, bf16[1024,128]{1,0:T(8,128)(2,1)S(1)} %get-tuple-element.17.k_ref, bf16[1024,128]{1,0:T(8,128)(2,1)S(1)} %get-tuple-element.18.v_ref, ...), custom_call_target="tpu_custom_call" | custom-call | tf_op jit(solution)/shard_map/pallas_call | solution.py:248
  (1 shorter events, 0.0 us)
Async XLA Ops:
  3.6 15.6 %collective-permute-start = (f32[192,128]{1,0:T(8,128)S(1)}, f32[192,128]{1,0:T(8,128)S(1)}, u32[]{:S(2)}, u32[]{:S(2)}) collective-permute-start(f32[192,128]{1,0:T(8,128)S(1)} %get-tuple-element.22), channel_id=1, source_target_pairs={{0,1},{1,0},{2,3},{3,2},{4,5},{5,4},{6,7},{7,6},{8,9},{9,8},{10,11... | collective-permute-start | bytes 294920 | tf_op jit(solution)/shard_map/ppermute | solution.py:236

commit v10 on v9

--- a/solution.py
+++ b/solution.py
@@ -123,23 +123,26 @@
     part = got_ref[width:, :]
     kv = own_ref[0] + jnp.where(side == 0, part, whole)
     back = own_ref[1] + jnp.where(side == 0, whole, part)
-    for i in range(count):
-        takes_kv = jnp.logical_or(i // 2 > me // 2, (i // 2 == me // 2) & (me % 2 == 0))
-        cut = slice((i % 2) * rows, (i % 2 + 1) * rows)
-        out_ref[i] = jnp.where(takes_kv, kv[cut], back[cut])
+    pairs = count // 2
+    for z in range(2):
+        cut = slice(z * rows, (z + 1) * rows)
+        for x in range(pairs):
+            takes_kv = jnp.logical_or(x > me // 2, (x == me // 2) & (me % 2 == 0))
+            out_ref[z * pairs + x] = jnp.where(takes_kv, kv[cut], back[cut])
 
 
 def gather_kernel(parts_ref, send_ref):
     pair = lax.axis_index("seq") // 2
     zero = jnp.zeros(parts_ref.shape[1:], F32)
     earlier, later = zero, zero
-    count = parts_ref.shape[0]
-    for i in range(count):
-        earlier = earlier + jnp.where(i // 2 < pair, parts_ref[i], zero)
-        j = count - 1 - i
-        later = later + jnp.where(j // 2 > pair, parts_ref[j], zero)
-    with_first = earlier + parts_ref[2 * pair]
-    with_second = later + parts_ref[2 * pair + 1]
+    pairs = parts_ref.shape[0] // 2
+    for x in range(pairs):
+        y = pairs - 1 - x
+        for z in range(2):
+            earlier = earlier + jnp.where(x < pair, parts_ref[z * pairs + x], zero)
+            later = later + jnp.where(y > pair, parts_ref[z * pairs + y], zero)
+    with_first = earlier + parts_ref[pair]
+    with_second = later + parts_ref[pairs + pair]
     for side in range(2):
         send_ref[side, 0] = earlier
         send_ref[side, 1] = with_second
@@ -211,7 +214,7 @@
     )
 
 
-def per_device(pairs, groups, queries, key_vectors, value_vectors, out_grad):
+def per_device(pairs, lines, groups, queries, key_vectors, value_vectors, out_grad):
     half_rows, width = queries.shape
     blocks = half_rows // BLOCK
     rows16 = jax.ShapeDtypeStruct((half_rows, width), BF16)
@@ -241,7 +244,7 @@
         jax.ShapeDtypeStruct((count, quarter, width), F32),
         2**23,
     )(own, got)
-    parts = lax.all_to_all(parts, "seq", 0, 0)
+    parts = lax.all_to_all(parts, AXES, 0, 0, axis_index_groups=lines)
     quads = jax.ShapeDtypeStruct((4, 2, quarter, width), F32)
     state = call(gather_kernel, quads, 2**23)(parts)
     state = lax.all_to_all(state, AXES, 0, 0, axis_index_groups=groups)
@@ -259,6 +262,10 @@
 def solution(mesh):
     n_seq, n_inner = mesh.shape["seq"], mesh.shape["inner"]
     pairs = [(i, i ^ 1) for i in range(n_seq * n_inner)]
+    lines = [
+        [(2 * x + z) * n_inner + i for z in range(2) for x in range(n_seq // 2)]
+        for i in range(n_inner)
+    ]
     groups = [
         [(2 * x + z) * n_inner + 2 * h + side for z in range(2) for side in range(2)]
         for x in range(n_seq // 2)
@@ -266,7 +273,7 @@
     ]
     spec = P("seq", "inner")
     return jax.shard_map(
-        functools.partial(per_device, pairs, groups),
+        functools.partial(per_device, pairs, lines, groups),
         mesh=mesh,
         in_specs=(spec,) * 4,
         out_specs=(spec,) * 4,

time: 42.8 us -> 41.7 us (0.974)
  the two profiles are of different devices: /device:TPU:1 before, /device:TPU:2 now
where the time goes in v10:
time: 41.7 us; the launch traced here: 41.5 us
  blocking collectives  33.4 us (80%)
  Pallas kernels  4.2 us (10%)
  starting transfers between devices  1.92 us (5%)
  waiting for transfers between devices  1.27 us (3%)
  between operations  0.66 us (2%)
    all_to_all x1, blocking collectives, per_device(): parts = lax.all_to_all(parts, AXES, 0, 0, axis_index_groups=lines)  26.3 us
    all_to_all x1, blocking collectives, per_device(): state = lax.all_to_all(state, AXES, 0, 0, axis_index_groups=groups)  7.12 us
    pallas_call x1, Pallas kernels, per_device(): call(final_kernel, (rows16,) * 4, 2 ** 24, out_specs=(in_hbm,) * 4, scrat...  2.52 us
    ppermute x1, starting transfers between devices, per_device(): got = lax.ppermute(send, AXES, pairs)  1.92 us
    pallas_call x1, Pallas kernels, per_device(): call(outer_kernel, (sent, halves, states) + (rows16,) * 4 + (rows32,) * 5...  1.59 us
    ppermute x1, waiting for transfers between devices, per_device(): got = lax.ppermute(send, AXES, pairs)  1.27 us
  transfers between devices with their start and end apart: 1, of which 1 were waited for; matrix products, arithmetic and copies ran while one was open for 0% of the time, Pallas kernels for 0%

profile of v10, /device:TPU:2, one launch (start us, length us, event | category | flops | bytes accessed | tf_op | source)
XLA Modules:
  0.0 41.5 jit_solution(3153598971159201528)
XLA Ops:
  0.6 1.6 %shard_map.75 = (f32[192,128]{1,0:T(8,128)S(1)}, f32[2,64,128]{2,1,0:T(8,128)S(1)}, f32[256,128]{1,0:T(8,128)S(1)}, bf16[1024,128]{1,0:T(8,128)(2,1)S(1)}, bf16[...) custom-call(bf16[1024,128]{1,0:T(8,128)(2,1)} %q_hbm.1, ...), custom_call_target="tpu_custom_call" | custom-call | tf_op jit(solution)/shard_map/pallas_call | solution.py:227
  2.2 1.9 %collective-permute-start = (f32[192,128]{1,0:T(8,128)S(1)}, f32[192,128]{1,0:T(8,128)S(1)}, u32[]{:S(2)}, u32[]{:S(2)}) collective-permute-start(f32[192,128]{1,0:T(8,128)S(1)} %get-tuple-element.22), channel_id=1, source_target_pairs={{0,1},{1,0},{2,3},{3,2},{4,5},{5,4},{6,7},{7,6},{8,9},{9,8},{10,11... | collective-permute-start | bytes 294920 | tf_op jit(solution)/shard_map/ppermute | solution.py:239
  4.2 1.3 %collective-permute-done.got_ref = f32[192,128]{1,0:T(8,128)S(1)} collective-permute-done((f32[192,128]{1,0:T(8,128)S(1)}, f32[192,128]{1,0:T(8,128)S(1)}, u32[]{:S(2)}, u32[]{:S(2)}) %collective-permute-start) | collective-permute-done | bytes 98336 | tf_op jit(solution)/shard_map/ppermute | solution.py:239
  5.5 26.3 %all_to_all.10.parts_ref = f32[16,32,128]{2,1,0:T(8,128)S(1)} all-to-all(f32[16,32,128]{2,1,0:T(8,128)S(1)} %shard_map.76), channel_id=1, replica_groups={{0,128,256,384,512,640,768,896,64,192,320,448,576,704,832,960},{1,129,2..., dimensions={0} | all-to-all | bytes 524288 | tf_op jit(solution)/shard_map/all_to_all | solution.py:247
  31.8 0.1 shard_map.77
  31.8 7.1 %all_to_all.11.state_ref = f32[4,2,32,128]{3,2,1,0:T(8,128)S(1)} all-to-all(f32[4,2,32,128]{3,2,1,0:T(8,128)S(1)} %shard_map.77), channel_id=1, replica_groups={{0,1,64,65},{2,3,66,67},{4,5,68,69},{6,7,70,71},{8,9,72,73},{10,11,74,7..., dimensions={0} | all-to-all | bytes 262144 | tf_op jit(solution)/shard_map/all_to_all | solution.py:250
  39.0 2.5 %shard_map.78 = (bf16[1024,128]{1,0:T(8,128)(2,1)}, bf16[1024,128]{1,0:T(8,128)(2,1)}, bf16[1024,128]{1,0:T(8,128)(2,1)}, bf16[1024,128]{1,0:T(8,128)(2,1)}) custom-call(bf16[1024,128]{1,0:T(8,128)(2,1)S(1)} %get-tuple-element.16.q_ref, bf16[1024,128]{1,0:T(8,128)(2,1)S(1)} %get-tuple-element.17.k_ref, bf16[1024,128]{1,0:T(8,128)(2,1)S(1)} %get-tuple-element.18.v_ref, ...), custom_call_target="tpu_custom_call" | custom-call | tf_op jit(solution)/shard_map/pallas_call | solution.py:251
  (1 shorter events, 0.0 us)
Async XLA Ops:
  2.2 3.2 %collective-permute-start = (f32[192,128]{1,0:T(8,128)S(1)}, f32[192,128]{1,0:T(8,128)S(1)}, u32[]{:S(2)}, u32[]{:S(2)}) collective-permute-start(f32[192,128]{1,0:T(8,128)S(1)} %get-tuple-element.22), channel_id=1, source_target_pairs={{0,1},{1,0},{2,3},{3,2},{4,5},{5,4},{6,7},{7,6},{8,9},{9,8},{10,11... | collective-permute-start | bytes 294920 | tf_op jit(solution)/shard_map/ppermute | solution.py:239

commit v11 on v10

--- a/solution.py
+++ b/solution.py
@@ -144,10 +144,10 @@
     with_first = earlier + parts_ref[pair]
     with_second = later + parts_ref[pairs + pair]
     for side in range(2):
-        send_ref[side, 0] = earlier
-        send_ref[side, 1] = with_second
-        send_ref[2 + side, 0] = with_first
-        send_ref[2 + side, 1] = later
+        send_ref[2 * side, 0] = earlier
+        send_ref[2 * side, 1] = with_second
+        send_ref[2 * side + 1, 0] = with_first
+        send_ref[2 * side + 1, 1] = later
 
 
 def final_kernel(
@@ -158,7 +158,7 @@
     half_rows, width = q_ref.shape
     is_second = lax.axis_index("inner") % 2 == 1
     kv0, back1 = (
-        jnp.concatenate([state_ref[2 * z + c, i] for c in range(2) for z in range(2)], 0)
+        jnp.concatenate([state_ref[j, i] for j in range(4)], 0)
         for i in range(2)
     )
     other = got_ref[:width, :]
@@ -267,7 +267,7 @@
         for i in range(n_inner)
     ]
     groups = [
-        [(2 * x + z) * n_inner + 2 * h + side for z in range(2) for side in range(2)]
+        [(2 * x + z) * n_inner + 2 * h + side for side in range(2) for z in range(2)]
         for x in range(n_seq // 2)
         for h in range(n_inner // 2)
     ]

time: 41.7 us -> 41.7 us (level)
  no operation moved by 1% of the time
where the time goes in v11:
time: 41.7 us; the launch traced here: 41.5 us
  blocking collectives  33.4 us (80%)
  Pallas kernels  4.2 us (10%)
  starting transfers between devices  1.92 us (5%)
  waiting for transfers between devices  1.27 us (3%)
  between operations  0.66 us (2%)
    all_to_all x1, blocking collectives, per_device(): parts = lax.all_to_all(parts, AXES, 0, 0, axis_index_groups=lines)  26.3 us
    all_to_all x1, blocking collectives, per_device(): state = lax.all_to_all(state, AXES, 0, 0, axis_index_groups=groups)  7.12 us
    pallas_call x1, Pallas kernels, per_device(): call(final_kernel, (rows16,) * 4, 2 ** 24, out_specs=(in_hbm,) * 4, scrat...  2.52 us
    ppermute x1, starting transfers between devices, per_device(): got = lax.ppermute(send, AXES, pairs)  1.92 us
    pallas_call x1, Pallas kernels, per_device(): call(outer_kernel, (sent, halves, states) + (rows16,) * 4 + (rows32,) * 5...  1.59 us
    ppermute x1, waiting for transfers between devices, per_device(): got = lax.ppermute(send, AXES, pairs)  1.27 us
  transfers between devices with their start and end apart: 1, of which 1 were waited for; matrix products, arithmetic and copies ran while one was open for 0% of the time, Pallas kernels for 0%

profile of v11, /device:TPU:2, one launch (start us, length us, event | category | flops | bytes accessed | tf_op | source)
XLA Modules:
  0.0 41.5 jit_solution(2886569080765931035)
XLA Ops:
  0.6 1.6 %shard_map.75 = (f32[192,128]{1,0:T(8,128)S(1)}, f32[2,64,128]{2,1,0:T(8,128)S(1)}, f32[256,128]{1,0:T(8,128)S(1)}, bf16[1024,128]{1,0:T(8,128)(2,1)S(1)}, bf16[...) custom-call(bf16[1024,128]{1,0:T(8,128)(2,1)} %q_hbm.1, ...), custom_call_target="tpu_custom_call" | custom-call | tf_op jit(solution)/shard_map/pallas_call | solution.py:227
  2.2 1.9 %collective-permute-start = (f32[192,128]{1,0:T(8,128)S(1)}, f32[192,128]{1,0:T(8,128)S(1)}, u32[]{:S(2)}, u32[]{:S(2)}) collective-permute-start(f32[192,128]{1,0:T(8,128)S(1)} %get-tuple-element.22), channel_id=1, source_target_pairs={{0,1},{1,0},{2,3},{3,2},{4,5},{5,4},{6,7},{7,6},{8,9},{9,8},{10,11... | collective-permute-start | bytes 294920 | tf_op jit(solution)/shard_map/ppermute | solution.py:239
  4.2 1.3 %collective-permute-done.got_ref = f32[192,128]{1,0:T(8,128)S(1)} collective-permute-done((f32[192,128]{1,0:T(8,128)S(1)}, f32[192,128]{1,0:T(8,128)S(1)}, u32[]{:S(2)}, u32[]{:S(2)}) %collective-permute-start) | collective-permute-done | bytes 98336 | tf_op jit(solution)/shard_map/ppermute | solution.py:239
  5.5 26.3 %all_to_all.10.parts_ref = f32[16,32,128]{2,1,0:T(8,128)S(1)} all-to-all(f32[16,32,128]{2,1,0:T(8,128)S(1)} %shard_map.76), channel_id=1, replica_groups={{0,128,256,384,512,640,768,896,64,192,320,448,576,704,832,960},{1,129,2..., dimensions={0} | all-to-all | bytes 524288 | tf_op jit(solution)/shard_map/all_to_all | solution.py:247
  31.8 0.1 shard_map.77
  31.8 7.1 %all_to_all.11.state_ref = f32[4,2,32,128]{3,2,1,0:T(8,128)S(1)} all-to-all(f32[4,2,32,128]{3,2,1,0:T(8,128)S(1)} %shard_map.77), channel_id=1, replica_groups={{0,64,1,65},{2,66,3,67},{4,68,5,69},{6,70,7,71},{8,72,9,73},{10,74,11,7..., dimensions={0} | all-to-all | bytes 262144 | tf_op jit(solution)/shard_map/all_to_all | solution.py:250
  39.0 2.5 %shard_map.78 = (bf16[1024,128]{1,0:T(8,128)(2,1)}, bf16[1024,128]{1,0:T(8,128)(2,1)}, bf16[1024,128]{1,0:T(8,128)(2,1)}, bf16[1024,128]{1,0:T(8,128)(2,1)}) custom-call(bf16[1024,128]{1,0:T(8,128)(2,1)S(1)} %get-tuple-element.16.q_ref, bf16[1024,128]{1,0:T(8,128)(2,1)S(1)} %get-tuple-element.17.k_ref, bf16[1024,128]{1,0:T(8,128)(2,1)S(1)} %get-tuple-element.18.v_ref, ...), custom_call_target="tpu_custom_call" | custom-call | tf_op jit(solution)/shard_map/pallas_call | solution.py:251
  (1 shorter events, 0.0 us)
Async XLA Ops:
  2.2 3.2 %collective-permute-start = (f32[192,128]{1,0:T(8,128)S(1)}, f32[192,128]{1,0:T(8,128)S(1)}, u32[]{:S(2)}, u32[]{:S(2)}) collective-permute-start(f32[192,128]{1,0:T(8,128)S(1)} %get-tuple-element.22), channel_id=1, source_target_pairs={{0,1},{1,0},{2,3},{3,2},{4,5},{5,4},{6,7},{7,6},{8,9},{9,8},{10,11... | collective-permute-start | bytes 294920 | tf_op jit(solution)/shard_map/ppermute | solution.py:239

commit v12 on v11

--- a/solution.py
+++ b/solution.py
@@ -128,7 +128,7 @@
         cut = slice(z * rows, (z + 1) * rows)
         for x in range(pairs):
             takes_kv = jnp.logical_or(x > me // 2, (x == me // 2) & (me % 2 == 0))
-            out_ref[z * pairs + x] = jnp.where(takes_kv, kv[cut], back[cut])
+            out_ref[z * pairs + pairs - 1 - x] = jnp.where(takes_kv, kv[cut], back[cut])
 
 
 def gather_kernel(parts_ref, send_ref):
@@ -139,10 +139,10 @@
     for x in range(pairs):
         y = pairs - 1 - x
         for z in range(2):
-            earlier = earlier + jnp.where(x < pair, parts_ref[z * pairs + x], zero)
-            later = later + jnp.where(y > pair, parts_ref[z * pairs + y], zero)
-    with_first = earlier + parts_ref[pair]
-    with_second = later + parts_ref[pairs + pair]
+            earlier = earlier + jnp.where(x < pair, parts_ref[z * pairs + y], zero)
+            later = later + jnp.where(y > pair, parts_ref[z * pairs + x], zero)
+    with_first = earlier + parts_ref[pairs - 1 - pair]
+    with_second = later + parts_ref[2 * pairs - 1 - pair]
     for side in range(2):
         send_ref[2 * side, 0] = earlier
         send_ref[2 * side, 1] = with_second
@@ -263,7 +263,7 @@
     n_seq, n_inner = mesh.shape["seq"], mesh.shape["inner"]
     pairs = [(i, i ^ 1) for i in range(n_seq * n_inner)]
     lines = [
-        [(2 * x + z) * n_inner + i for z in range(2) for x in range(n_seq // 2)]
+        [(2 * x + z) * n_inner + i for z in range(2) for x in reversed(range(n_seq // 2))]
         for i in range(n_inner)
     ]
     groups = [

time: 41.7 us -> 41.5 us (level)
  the two profiles are of different devices: /device:TPU:2 before, /device:TPU:1 now
where the time goes in v12:
time: 41.5 us; the launch traced here: 41.3 us
  blocking collectives  20.7 us (50%)
  starting transfers between devices  14.7 us (35%)
  Pallas kernels  4.36 us (11%)
  waiting for transfers between devices  0.92 us (2%)
  between operations  0.66 us (2%)
    ppermute x1, starting transfers between devices, per_device(): got = lax.ppermute(send, AXES, pairs)  14.7 us
    all_to_all x1, blocking collectives, per_device(): parts = lax.all_to_all(parts, AXES, 0, 0, axis_index_groups=lines)  12.3 us
    all_to_all x1, blocking collectives, per_device(): state = lax.all_to_all(state, AXES, 0, 0, axis_index_groups=groups)  8.43 us
    pallas_call x1, Pallas kernels, per_device(): call(outer_kernel, (sent, halves, states) + (rows16,) * 4 + (rows32,) * 5...  2.99 us
    pallas_call x1, Pallas kernels, per_device(): call(final_kernel, (rows16,) * 4, 2 ** 24, out_specs=(in_hbm,) * 4, scrat...  1.28 us
    ppermute x1, waiting for transfers between devices, per_device(): got = lax.ppermute(send, AXES, pairs)  0.92 us
  transfers between devices with their start and end apart: 1, of which 1 were waited for; matrix products, arithmetic and copies ran while one was open for 0% of the time, Pallas kernels for 0%

profile of v12, /device:TPU:1, one launch (start us, length us, event | category | flops | bytes accessed | tf_op | source)
XLA Modules:
  0.0 41.3 jit_solution(6575073789494584968)
XLA Ops:
  0.6 3.0 %shard_map.75 = (f32[192,128]{1,0:T(8,128)S(1)}, f32[2,64,128]{2,1,0:T(8,128)S(1)}, f32[256,128]{1,0:T(8,128)S(1)}, bf16[1024,128]{1,0:T(8,128)(2,1)S(1)}, bf16[...) custom-call(bf16[1024,128]{1,0:T(8,128)(2,1)} %q_hbm.1, ...), custom_call_target="tpu_custom_call" | custom-call | tf_op jit(solution)/shard_map/pallas_call | solution.py:227
  3.6 14.7 %collective-permute-start = (f32[192,128]{1,0:T(8,128)S(1)}, f32[192,128]{1,0:T(8,128)S(1)}, u32[]{:S(2)}, u32[]{:S(2)}) collective-permute-start(f32[192,128]{1,0:T(8,128)S(1)} %get-tuple-element.22), channel_id=1, source_target_pairs={{0,1},{1,0},{2,3},{3,2},{4,5},{5,4},{6,7},{7,6},{8,9},{9,8},{10,11... | collective-permute-start | bytes 294920 | tf_op jit(solution)/shard_map/ppermute | solution.py:239
  18.3 0.9 %collective-permute-done.got_ref = f32[192,128]{1,0:T(8,128)S(1)} collective-permute-done((f32[192,128]{1,0:T(8,128)S(1)}, f32[192,128]{1,0:T(8,128)S(1)}, u32[]{:S(2)}, u32[]{:S(2)}) %collective-permute-start) | collective-permute-done | bytes 98336 | tf_op jit(solution)/shard_map/ppermute | solution.py:239
  19.3 12.3 %all_to_all.10.parts_ref = f32[16,32,128]{2,1,0:T(8,128)S(1)} all-to-all(f32[16,32,128]{2,1,0:T(8,128)S(1)} %shard_map.76), channel_id=1, replica_groups={{896,768,640,512,384,256,128,0,960,832,704,576,448,320,192,64},{897,769..., dimensions={0} | all-to-all | bytes 524288 | tf_op jit(solution)/shard_map/all_to_all | solution.py:247
  31.5 0.1 shard_map.77
  31.6 8.4 %all_to_all.11.state_ref = f32[4,2,32,128]{3,2,1,0:T(8,128)S(1)} all-to-all(f32[4,2,32,128]{3,2,1,0:T(8,128)S(1)} %shard_map.77), channel_id=1, replica_groups={{0,64,1,65},{2,66,3,67},{4,68,5,69},{6,70,7,71},{8,72,9,73},{10,74,11,7..., dimensions={0} | all-to-all | bytes 262144 | tf_op jit(solution)/shard_map/all_to_all | solution.py:250
  40.0 1.3 %shard_map.78 = (bf16[1024,128]{1,0:T(8,128)(2,1)}, bf16[1024,128]{1,0:T(8,128)(2,1)}, bf16[1024,128]{1,0:T(8,128)(2,1)}, bf16[1024,128]{1,0:T(8,128)(2,1)}) custom-call(bf16[1024,128]{1,0:T(8,128)(2,1)S(1)} %get-tuple-element.16.q_ref, bf16[1024,128]{1,0:T(8,128)(2,1)S(1)} %get-tuple-element.17.k_ref, bf16[1024,128]{1,0:T(8,128)(2,1)S(1)} %get-tuple-element.18.v_ref, ...), custom_call_target="tpu_custom_call" | custom-call | tf_op jit(solution)/shard_map/pallas_call | solution.py:251
  (1 shorter events, 0.0 us)
Async XLA Ops:
  3.6 15.6 %collective-permute-start = (f32[192,128]{1,0:T(8,128)S(1)}, f32[192,128]{1,0:T(8,128)S(1)}, u32[]{:S(2)}, u32[]{:S(2)}) collective-permute-start(f32[192,128]{1,0:T(8,128)S(1)} %get-tuple-element.22), channel_id=1, source_target_pairs={{0,1},{1,0},{2,3},{3,2},{4,5},{5,4},{6,7},{7,6},{8,9},{9,8},{10,11... | collective-permute-start | bytes 294920 | tf_op jit(solution)/shard_map/ppermute | solution.py:239
